TPU v7x, 256 devices: a whole 4x4x8 slice. The times are simulated.
256 devices in a mesh: dp: 32 (over y, x, core), tensor: 8 (over z).
Axes of the slice: x: 4, y: 4, z: 8, core: 2. Of those that a mesh axis runs over, the one named last changes fastest.
Arguments:
- patches: bfloat16 [49152, 1280], P('dp', 'tensor'), may hold values from -6 to 6
- gain: float32 [1280], replicated, may hold values from 0.25 to 1.75
- window_dest: int32 [768], P('dp'), may hold values from -1 to 31, as said below
- window_pos: int32 [768], P('dp'), may hold values from -1 to 16368, as said below
- fc1: bfloat16 [5120, 2560], P('dp', 'tensor'), may hold values from -0.078125 to 0.078125
- fc2: bfloat16 [2560, 8192], P('dp', 'tensor'), may hold values from -0.125 to 0.125
- text_embeds: bfloat16 [16384, 8192], P('dp', 'tensor'), may hold values from -6 to 6
- lm_grad: bfloat16 [16384, 8192], P('dp', 'tensor'), may hold values from -0.046875 to 0.046875
Outputs:
- lm_embeds: bfloat16 [16384, 8192], P('dp', 'tensor')
- grad_fc1: float32 [5120, 2560], P('dp', 'tensor')
- grad_fc2: float32 [2560, 8192], P('dp', 'tensor')
Inputs may be any that keep to these rules, and one draw needn't show every extreme that they name: `window_dest`: live slots come first on each index of dp, which holds 8 or 24 of them. Every index of dp is named by exactly 16 live slots; the slots of one index of dp name one index at most 1 times, and some index of dp reaches that. `window_pos`: -1 exactly where window_dest is -1. The 16 rows from window_pos of a live slot lie in one block of 512 rows (one index of dp), never intersection another slot's rows, and every such block receives exactly 16 windows; at most 1 windows of one block share one value of window_dest, and some block reaches that.
All inputs are finite; a program needn't handle non-finite values.
Results may differ from a plain program's by a relative error of at most 0.029.
Values may be sent and summed in bfloat16 or wider, within the bound.
A program may use at most 128 MiB of HBM per device.

v0:
```python
import jax
import jax.numpy as jnp
from jax import lax
from jax.sharding import PartitionSpec as P

DH = 5120
WIN = 64
TOKW = 16
WORK_WIN = 16
SRC_WIN = 24


def gelu_slope(z):
    cdf = 0.5 * (1.0 + lax.erf(z * 0.7071067811865476))
    pdf = jnp.exp(-0.5 * z * z) * 0.3989422804014327
    return cdf + z * pdf


def slot_table(targets, peers, places, capacity):
    counts = jnp.arange(capacity, dtype=jnp.int32)
    match = (targets[None, None, :] == peers[:, None, None]) & (
        places[None, None, :] == counts[None, :, None]
    )
    items = jnp.arange(targets.shape[0], dtype=jnp.int32)
    picked = jnp.sum(jnp.where(match, items[None, None, :], 0), axis=2)
    return (picked, jnp.any(match, axis=2))


def earlier_same(targets):
    items = jnp.arange(targets.shape[0], dtype=jnp.int32)
    same = (targets[:, None] == targets[None, :]) & (items[None, :] < items[:, None])
    return jnp.sum(same, axis=1)


def per_device(patches, gain, window_dest, window_pos, fc1, fc2, text_embeds, lm_grad):
    dp_count = lax.axis_size("dp")
    feat_local = patches.shape[1]
    lm_rows, out_local = text_embeds.shape
    tok_rows = WORK_WIN * TOKW
    cap_in = (SRC_WIN + dp_count - 1) // dp_count
    cap_out = (WORK_WIN + dp_count - 1) // dp_count
    peers = jnp.arange(dp_count, dtype=jnp.int32)
    picked, used = slot_table(window_dest, peers, earlier_same(window_dest), cap_in)
    slot_rows = patches.reshape(SRC_WIN, WIN * feat_local)
    outgoing = jnp.where(used[:, :, None], slot_rows[picked], jnp.zeros((), jnp.bfloat16))
    sent_pos = jnp.where(used, window_pos[picked], -1)
    arrived, arrived_pos = (
        lax.all_to_all(outgoing, "dp", split_axis=0, concat_axis=0, tiled=True),
        lax.all_to_all(sent_pos, "dp", split_axis=0, concat_axis=0, tiled=True),
    )
    flat = arrived.reshape(dp_count * cap_in, WIN * feat_local)
    flat_pos = arrived_pos.reshape(-1)
    live = flat_pos >= 0
    ranks = jnp.cumsum(live.astype(jnp.int32)) - 1
    wanted = jnp.arange(WORK_WIN, dtype=jnp.int32)
    entries = jnp.arange(dp_count * cap_in, dtype=jnp.int32)
    hits = live[None, :] & (ranks[None, :] == wanted[:, None])
    chosen = jnp.sum(jnp.where(hits, entries[None, :], 0), axis=1)
    work = flat[chosen].reshape(WORK_WIN, WIN, feat_local)
    work_pos = flat_pos[chosen]
    full = lax.all_gather(work, "tensor", axis=2, tiled=True)
    values = full.astype(jnp.float32)
    scale = lax.rsqrt(jnp.mean(values * values, axis=-1, keepdims=True) + 1e-06)
    normed = (values * scale * gain).astype(jnp.bfloat16).reshape(tok_rows, DH)
    columns = normed
    first = jnp.dot(
        columns, lax.all_gather(fc1, "dp", axis=0, tiled=True), preferred_element_type=jnp.float32
    )
    hidden = jax.nn.gelu(first, approximate=False).astype(jnp.bfloat16)
    hidden_full = lax.all_gather(hidden, "tensor", axis=1, tiled=True)
    columns = hidden_full
    mixed = jnp.dot(
        columns, lax.all_gather(fc2, "dp", axis=0, tiled=True), preferred_element_type=jnp.float32
    )
    merged = mixed.astype(jnp.bfloat16)
    owner = (work_pos // lm_rows).astype(jnp.int32)
    place = earlier_same(owner)
    pick_out, used_out = slot_table(owner, peers, place, cap_out)
    blocks = merged.reshape(WORK_WIN, TOKW * out_local)
    parcel = jnp.where(used_out[:, :, None], blocks[pick_out], jnp.zeros((), jnp.bfloat16))
    parcel_pos = jnp.where(used_out, work_pos[pick_out], -1)
    got, got_pos = (
        lax.all_to_all(parcel, "dp", split_axis=0, concat_axis=0, tiled=True),
        lax.all_to_all(parcel_pos, "dp", split_axis=0, concat_axis=0, tiled=True),
    )
    base = lax.axis_index("dp") * lm_rows
    offsets = jnp.arange(TOKW, dtype=jnp.int32)
    token_rows = jnp.where(
        got_pos[:, :, None] >= 0, got_pos[:, :, None] - base + offsets[None, None, :], -1
    ).reshape(-1)
    row_ids = jnp.arange(lm_rows, dtype=jnp.int32)
    table = row_ids[:, None] == token_rows[None, :]
    incoming = got.reshape(dp_count * cap_out * TOKW, out_local)
    placed = jnp.dot(table.astype(jnp.bfloat16), incoming, preferred_element_type=jnp.float32)
    covered = jnp.any(table, axis=1)
    lm_embeds = jnp.where(covered[:, None], placed.astype(jnp.bfloat16), text_embeds)
    returned = lax.dot_general(
        table.astype(jnp.bfloat16),
        lm_grad,
        (((0,), (0,)), ((), ())),
        preferred_element_type=jnp.float32,
    )
    returned = returned.astype(jnp.bfloat16).reshape(dp_count, cap_out, TOKW * out_local)
    back = lax.all_to_all(returned, "dp", split_axis=0, concat_axis=0, tiled=True)
    upstream = back[owner, place].reshape(tok_rows, out_local)
    columns = hidden_full
    grad_fc2 = lax.psum_scatter(
        lax.dot_general(
            columns, upstream, (((0,), (0,)), ((), ())), preferred_element_type=jnp.float32
        ).astype(jnp.bfloat16),
        "dp",
        scatter_dimension=0,
        tiled=True,
    ).astype(jnp.float32)
    second_full = lax.all_gather(fc2, "dp", axis=0, tiled=True)
    hidden_back = lax.psum_scatter(
        lax.dot_general(
            second_full, upstream, (((1,), (1,)), ((), ())), preferred_element_type=jnp.float32
        ).astype(jnp.bfloat16),
        "tensor",
        scatter_dimension=0,
        tiled=True,
    ).astype(jnp.float32)
    slope = (hidden_back.T * gelu_slope(first)).astype(jnp.bfloat16)
    columns = normed
    grad_fc1 = lax.psum_scatter(
        lax.dot_general(
            columns, slope, (((0,), (0,)), ((), ())), preferred_element_type=jnp.float32
        ).astype(jnp.bfloat16),
        "dp",
        scatter_dimension=0,
        tiled=True,
    ).astype(jnp.float32)
    return (lm_embeds, grad_fc1, grad_fc2)


def solution(mesh):
    in_specs = (
        P("dp", "tensor"),
        P(),
        P("dp"),
        P("dp"),
        P("dp", "tensor"),
        P("dp", "tensor"),
        P("dp", "tensor"),
        P("dp", "tensor"),
    )
    out_specs = (P("dp", "tensor"), P("dp", "tensor"), P("dp", "tensor"))
    return jax.shard_map(
        per_device, mesh=mesh, in_specs=in_specs, out_specs=out_specs, check_vma=False
    )
```

profile of v0, /device:TPU:2, one launch (start us, length us, event | category | flops | bytes accessed | tf_op | source)
XLA Modules:
  0.0 500.0 jit_solution(1056775111840299021)
XLA Ops:
  11.7 7.6 %all-to-all-start = ((s32[32,1,1]{2,1,0:T(1,128)}), s32[32,1,1]{2,1,0:T(1,128)S(1)}, u32[]{:S(2)}, u32[]{:S(2)}) async-start(s32[32,1,1]{2,1,0:T(1,128)} %copy.40), calls=%async_computation | async-start | bytes 32768 | tf_op jit(solution)/shard_map/all_to_all | solution.py:49
  25.9 7.4 %all-to-all-start.2 = ((bf16[32,2,5120]{2,1,0:T(2,128)(2,1)}), bf16[32,2,5120]{2,1,0:T(2,128)(2,1)S(1)}, u32[]{:S(2)}, u32[]{:S(2)}) async-start(bf16[32,2,5120]{2,1,0:T(2,128)(2,1)} %reshape.692), calls=%async_computation.2 | async-start | bytes 1310720 | tf_op jit(solution)/shard_map/all_to_all | solution.py:48
  34.5 10.7 %all-to-all-done.2 = bf16[32,2,5120]{2,1,0:T(2,128)(2,1)S(1)} async-done(((bf16[32,2,5120]{2,1,0:T(2,128)(2,1)}), bf16[32,2,5120]{2,1,0:T(2,128)(2,1)S(1)}, u32[]{:S(2)}, u32[]{:S(2)}) %all-to-all-start.2) | async-done | bytes 655392 | tf_op jit(solution)/shard_map/all_to_all | solution.py:48
  52.9 5.0 %all-to-all-start.1 = ((s32[32,1,1]{2,1,0:T(1,128)}), s32[32,1,1]{2,1,0:T(1,128)S(1)}, u32[]{:S(2)}, u32[]{:S(2)}) async-start(s32[32,1,1]{2,1,0:T(1,128)} %copy.43), calls=%async_computation.1 | async-start | bytes 32768 | tf_op jit(solution)/shard_map/all_to_all | solution.py:84
  58.3 5.8 %all-to-all-done.1 = s32[32,1,1]{2,1,0:T(1,128)S(1)} async-done(((s32[32,1,1]{2,1,0:T(1,128)}), s32[32,1,1]{2,1,0:T(1,128)S(1)}, u32[]{:S(2)}, u32[]{:S(2)}) %all-to-all-start.1) | async-done | bytes 160 | tf_op jit(solution)/shard_map/all_to_all | solution.py:84
  64.2 49.7 %all-gather.5.cloned.1.call-done = bf16[16,64,1280]{1,0,2:T(8,128)(2,1)} async-done(((bf16[16,64,160]{1,0,2:T(8,128)(2,1)}), bf16[16,64,1280]{1,0,2:T(8,128)(2,1)}) %all-gather.5.cloned.1.call-update) | async-done | bytes 2621456 | tf_op jit(solution)/shard_map/all_gather | solution.py:61
  113.9 3.5 fusion
  118.0 4.9 fusion.2
  122.9 7.2 %copy.48 = bf16[16,64,1280]{2,1,0:T(8,128)(2,1)} copy(bf16[16,64,1280]{1,0,2:T(8,128)(2,1)} %fusion.2) | data formatting | bytes 5242880 | tf_op jit(solution)/shard_map/convert_element_type | solution.py:64
  130.1 5.2 %reshape.621 = bf16[256,5120]{1,0:T(8,128)(2,1)} reshape(bf16[16,64,1280]{2,1,0:T(8,128)(2,1)} %copy.48) | data formatting | bytes 5242880 | tf_op jit(solution)/shard_map/reshape | solution.py:64
  135.3 30.2 %all-gather.7.cloned.1.call-done = bf16[5120,320]{1,0:T(8,128)(2,1)} async-done(((bf16[160,320]{1,0:T(8,128)(2,1)}), bf16[5120,320]{1,0:T(8,128)(2,1)}) %all-gather.7.cloned.1.call-update) | async-done | bytes 3276816 | tf_op jit(solution)/shard_map/all_gather | solution.py:67
  165.6 5.7 %fusion.10 = (bf16[256,320]{0,1:T(8,128)(2,1)}, f32[256,320]{0,1:T(8,128)S(1)}) fusion(bf16[256,5120]{1,0:T(8,128)(2,1)} %reshape.621, bf16[5120,320]{1,0:T(8,128)(2,1)} %all-gather.7.cloned.1.call-done), kind=kOutput, calls=%fused_computation.31 | convolution fusion | flops 844185600 | bytes 6389760 | tf_op jit(solution)/shard_map/dot_general | solution.py:66
  172.1 1.7 convolution_convert_fusion.3
  173.9 4.7 reshape.687
  178.6 7.3 %reduce.12 = bf16[32,16384]{1,0:T(8,128)(2,1)S(1)} reduce(bf16[32,1,16384]{2,1,0:T(2,128)(2,1)S(1)} %reshape.687, bf16[]{:T(256)} %broadcast.613), dimensions={1}, to_apply=%reshape.687.reduce_sub_computation | reduce | bytes 2097154 | tf_op jit(solution)/shard_map/reshape | solution.py:103
  187.5 5.9 %all-to-all-start.4 = ((bf16[32,2,8192]{2,1,0:T(2,128)(2,1)}), bf16[32,2,8192]{2,1,0:T(2,128)(2,1)S(1)}, u32[]{:S(2)}, u32[]{:S(2)}) async-start(bf16[32,2,8192]{2,1,0:T(2,128)(2,1)} %reshape.696), calls=%async_computation.4 | async-start | bytes 2097152 | tf_op jit(solution)/shard_map/all_to_all | solution.py:104
  193.5 17.5 %all-to-all-done.4 = bf16[32,2,8192]{2,1,0:T(2,128)(2,1)S(1)} async-done(((bf16[32,2,8192]{2,1,0:T(2,128)(2,1)}), bf16[32,2,8192]{2,1,0:T(2,128)(2,1)S(1)}, u32[]{:S(2)}, u32[]{:S(2)}) %all-to-all-start.4) | async-done | bytes 1048608 | tf_op jit(solution)/shard_map/all_to_all | solution.py:104
  213.3 2.1 gather_fusion.6
  215.7 6.3 %all-gather.11.cloned.1.call-done = bf16[2560,1024]{1,0:T(8,128)(2,1)} async-done(((bf16[80,1024]{1,0:T(8,128)(2,1)}), bf16[2560,1024]{1,0:T(8,128)(2,1)}) %all-gather.11.cloned.1.call-update) | async-done | bytes 5242896 | tf_op jit(solution)/shard_map/all_gather | solution.py:73
  222.0 5.1 %fusion.3 = bf16[2560,256]{1,0:T(8,128)(2,1)} fusion(bf16[256,1024]{1,0:T(8,128)(2,1)S(1)} %reshape.625, bf16[2560,1024]{1,0:T(8,128)(2,1)} %all-gather.11.cloned.1.call-done), kind=kOutput, calls=%fused_computation.15 | convolution fusion | flops 1342832640 | bytes 7077888 | tf_op jit(solution)/shard_map/dot_general | solution.py:117
  227.2 36.1 %all-gather.9.cloned.1.call-done = bf16[256,2560]{0,1:T(8,128)(2,1)} async-done(((bf16[256,320]{0,1:T(8,128)(2,1)}), bf16[256,2560]{0,1:T(8,128)(2,1)}) %all-gather.9.cloned.1.call-update) | async-done | bytes 1310736 | tf_op jit(solution)/shard_map/all_gather | solution.py:70
  263.3 5.2 %convolution_convert_fusion.1 = bf16[2560,1024]{1,0:T(8,128)(2,1)} fusion(bf16[256,2560]{0,1:T(8,128)(2,1)} %all-gather.9.cloned.1.call-done, bf16[256,1024]{1,0:T(8,128)(2,1)S(1)} %reshape.625), kind=kOutput, calls=%fused_computation.13 | convolution fusion | flops 1344798720 | bytes 7077888 | tf_op jit(solution)/shard_map/dot_general | solution.py:108
  269.8 4.0 convolution_convert_fusion.5
  275.3 28.2 %reduce-scatter.4.cloned.1.call-done = bf16[320,256]{1,0:T(8,128)(2,1)} async-done(((bf16[2560,256]{1,0:T(8,128)(2,1)}), bf16[320,256]{1,0:T(8,128)(2,1)}) %reduce-scatter.4.cloned.1.call-update) | async-done | bytes 163856 | tf_op jit(solution)/shard_map/reduce_scatter | solution.py:116
  303.6 5.3 %convolution_convert_fusion = bf16[5120,320]{1,0:T(8,128)(2,1)} fusion(bf16[256,5120]{1,0:T(8,128)(2,1)} %reshape.621, f32[256,320]{0,1:T(8,128)S(1)} %get-tuple-element.4, bf16[320,256]{1,0:T(8,128)(2,1)} %reduce-scatter.4.cloned.1.call-done), kind=kOutput, calls=%fused_computation.12 | convolution fusion | flops 841400320 | bytes 6389760 | tf_op jit(solution)/shard_map/dot_general | solution.py:127
  312.1 7.7 %all-to-all-start.3 = ((bf16[32,2,8192]{2,1,0:T(2,128)(2,1)}), bf16[32,2,8192]{2,1,0:T(2,128)(2,1)S(1)}, u32[]{:S(2)}, u32[]{:S(2)}) async-start(bf16[32,2,8192]{2,1,0:T(2,128)(2,1)} %reshape.694), calls=%async_computation.3 | async-start | bytes 2097152 | tf_op jit(solution)/shard_map/all_to_all | solution.py:83
  320.0 15.8 %all-to-all-done.3 = bf16[32,2,8192]{2,1,0:T(2,128)(2,1)S(1)} async-done(((bf16[32,2,8192]{2,1,0:T(2,128)(2,1)}), bf16[32,2,8192]{2,1,0:T(2,128)(2,1)S(1)}, u32[]{:S(2)}, u32[]{:S(2)}) %all-to-all-start.3) | async-done | bytes 1048608 | tf_op jit(solution)/shard_map/all_to_all | solution.py:83
  336.8 7.4 %reduce.7 = bf16[32,16384]{1,0:T(8,128)(2,1)} reduce(bf16[32,1,16384]{2,1,0:T(2,128)(2,1)S(1)} %reshape.695, bf16[]{:T(256)} %constant.136), dimensions={1}, to_apply=%all_to_all.20.reduce_sub_computation | reduce | bytes 2097154 | tf_op jit(solution)/shard_map/all_to_all | solution.py:83
  345.8 2.9 fusion.4
  348.7 49.4 %reduce-scatter.8.cloned.1.call-done = bf16[80,1024]{1,0:T(8,128)(2,1)} async-done(((bf16[2560,1024]{1,0:T(8,128)(2,1)}), bf16[80,1024]{1,0:T(8,128)(2,1)}) %reduce-scatter.8.cloned.1.call-update) | async-done | bytes 163856 | tf_op jit(solution)/shard_map/reduce_scatter | solution.py:107
  398.1 1.7 convert_element_type.79
  399.8 91.5 %reduce-scatter.6.cloned.1.call-done = bf16[160,320]{1,0:T(8,128)(2,1)} async-done(((bf16[5120,320]{1,0:T(8,128)(2,1)}), bf16[160,320]{1,0:T(8,128)(2,1)}) %reduce-scatter.6.cloned.1.call-update) | async-done | bytes 102416 | tf_op jit(solution)/shard_map/reduce_scatter | solution.py:126
  (87 shorter events, 36.3 us)
Async XLA Ops:
  7.2 165.0 %copy-start = (bf16[512,1024]{1,0:T(8,128)(2,1)S(1)}, bf16[512,1024]{1,0:T(8,128)(2,1)}, u32[]{:S(2)}) copy-start(bf16[512,1024]{1,0:T(8,128)(2,1)} %param.15) | copy-start | bytes 3145732
  11.7 14.2 %all-to-all-start = ((s32[32,1,1]{2,1,0:T(1,128)}), s32[32,1,1]{2,1,0:T(1,128)S(1)}, u32[]{:S(2)}, u32[]{:S(2)}) async-start(s32[32,1,1]{2,1,0:T(1,128)} %copy.40), calls=%async_computation | async-start | bytes 32768 | tf_op jit(solution)/shard_map/all_to_all | solution.py:49
  25.9 19.3 %all-to-all-start.2 = ((bf16[32,2,5120]{2,1,0:T(2,128)(2,1)}), bf16[32,2,5120]{2,1,0:T(2,128)(2,1)S(1)}, u32[]{:S(2)}, u32[]{:S(2)}) async-start(bf16[32,2,5120]{2,1,0:T(2,128)(2,1)} %reshape.692), calls=%async_computation.2 | async-start | bytes 1310720 | tf_op jit(solution)/shard_map/all_to_all | solution.py:48
  33.3 80.6 %all-gather.5.cloned.1.call-start = ((), (), s32[]{:S(2)}) async-start(), calls=%async_computation.8 | async-start | bytes 5898240 | tf_op jit(solution)/shard_map/all_gather | solution.py:61
  48.9 68.5 %copy-start.4 = (f32[1280]{0:T(1024)S(1)}, f32[1280]{0:T(1024)}, u32[]{:S(2)}) copy-start(f32[1280]{0:T(1024)} %param.9) | copy-start | bytes 15364
  49.0 116.6 %all-gather.7.cloned.1.call-start = ((), (), s32[]{:S(2)}) async-start(), calls=%async_computation.9 | async-start | bytes 4055040 | tf_op jit(solution)/shard_map/all_gather | solution.py:67
  49.7 172.3 %all-gather.11.cloned.1.call-start = ((), (), s32[]{:S(2)}) async-start(), calls=%async_computation.11 | async-start | bytes 5406720 | tf_op jit(solution)/shard_map/all_gather | solution.py:73
  52.9 11.2 %all-to-all-start.1 = ((s32[32,1,1]{2,1,0:T(1,128)}), s32[32,1,1]{2,1,0:T(1,128)S(1)}, u32[]{:S(2)}, u32[]{:S(2)}) async-start(s32[32,1,1]{2,1,0:T(1,128)} %copy.43), calls=%async_computation.1 | async-start | bytes 32768 | tf_op jit(solution)/shard_map/all_to_all | solution.py:84
  58.0 205.3 %all-gather.9.cloned.1.call-start = ((), (), s32[]{:S(2)}) async-start(), calls=%async_computation.10 | async-start | bytes 1474560 | tf_op jit(solution)/shard_map/all_gather | solution.py:70
  113.9 4.1 copy-start.2
  187.5 23.5 %all-to-all-start.4 = ((bf16[32,2,8192]{2,1,0:T(2,128)(2,1)}), bf16[32,2,8192]{2,1,0:T(2,128)(2,1)S(1)}, u32[]{:S(2)}, u32[]{:S(2)}) async-start(bf16[32,2,8192]{2,1,0:T(2,128)(2,1)} %reshape.696), calls=%async_computation.4 | async-start | bytes 2097152 | tf_op jit(solution)/shard_map/all_to_all | solution.py:104
  193.4 110.2 %reduce-scatter.4.cloned.1.call-start = ((), (), s32[]{:S(2)}) async-start(), calls=%async_computation.12 | async-start | bytes 1474560 | tf_op jit(solution)/shard_map/reduce_scatter | solution.py:116
  227.1 171.0 %reduce-scatter.8.cloned.1.call-start = ((), (), s32[]{:S(2)}) async-start(), calls=%async_computation.14 | async-start | bytes 5406720 | tf_op jit(solution)/shard_map/reduce_scatter | solution.py:107
  268.5 1.3 copy-start.3
  268.5 222.8 %reduce-scatter.6.cloned.1.call-start = ((), (), s32[]{:S(2)}) async-start(), calls=%async_computation.13 | async-start | bytes 4055040 | tf_op jit(solution)/shard_map/reduce_scatter | solution.py:126
  312.1 23.7 %all-to-all-start.3 = ((bf16[32,2,8192]{2,1,0:T(2,128)(2,1)}), bf16[32,2,8192]{2,1,0:T(2,128)(2,1)S(1)}, u32[]{:S(2)}, u32[]{:S(2)}) async-start(bf16[32,2,8192]{2,1,0:T(2,128)(2,1)} %reshape.694), calls=%async_computation.3 | async-start | bytes 2097152 | tf_op jit(solution)/shard_map/all_to_all | solution.py:83
  336.8 156.1 %copy-start.1 = (bf16[512,1024]{1,0:T(8,128)(2,1)S(1)}, bf16[512,1024]{1,0:T(8,128)(2,1)}, u32[]{:S(2)}) copy-start(bf16[512,1024]{1,0:T(8,128)(2,1)} %param.15) | copy-start | bytes 3145732
Sparse Core Ops, SparseCore 0:
  49.1 64.7 all-gather.4
  116.5 49.0 all-gather.6
  168.1 53.8 all-gather.10
  224.2 39.0 all-gather.8
  265.7 37.8 reduce-scatter.3
  307.4 90.6 reduce-scatter.7
  402.6 88.6 reduce-scatter.5
where the time goes:
time: 507 us; the launch traced here: 500 us
  waiting for transfers between devices  343 us (68%)
  local copies, waits for them, and re-layouts  44.2 us (9%)
  starting transfers between devices  34.2 us (7%)
  other arithmetic  34.1 us (7%)
  matrix products  30 us (6%)
  between operations  14.7 us (3%)
    reduce_scatter x1, waiting for transfers between devices, per_device(): lax.psum_scatter(lax.dot_general(columns, slope, (((0,), (0,)), ((), ()))...  91.5 us
    all_gather x1, waiting for transfers between devices, per_device(): full = lax.all_gather(work, 'tensor', axis=2, tiled=True)  49.7 us
    reduce_scatter x1, waiting for transfers between devices, per_device(): lax.psum_scatter(lax.dot_general(columns, upstream, (((0,), (0,)), ((), (...  49.4 us
    all_gather x1, waiting for transfers between devices, per_device(): hidden_full = lax.all_gather(hidden, 'tensor', axis=1, tiled=True)  36.1 us
    all_gather x1, waiting for transfers between devices, per_device(): lax.all_gather(fc1, 'dp', axis=0, tiled=True)  30.2 us
    reduce_scatter x1, waiting for transfers between devices, per_device(): lax.psum_scatter(lax.dot_general(second_full, upstream, (((1,), (1,)), ((...  28.2 us
    all_to_all x1, waiting for transfers between devices, per_device(): lax.all_to_all(returned, 'dp', split_axis=0, concat_axis=0, tiled=True)  17.5 us
    all_to_all x1, waiting for transfers between devices, per_device(): lax.all_to_all(parcel, 'dp', split_axis=0, concat_axis=0, tiled=True)  15.8 us
  transfers between devices with their start and end apart: 12, of which 11 were waited for; matrix products, arithmetic and copies ran while one was open for 19% of the time, Pallas kernels for 0%

commit v1 on v0

v1 whole, which is shorter than its diff:
```python
import functools

import jax
import jax.numpy as jnp
from jax import lax
from jax.experimental import pallas as pl
from jax.experimental.pallas import tpu as pltpu
from jax.sharding import PartitionSpec as P

MESH = pl.DeviceIdType.MESH
BF = jnp.bfloat16
F32 = jnp.float32
DM = 1280
NDP = 32
NZ = 8
SRC = 24
WORK = 16
TOK = 16
FEAT = 640
WIDE = 768
HID = 320
HPAD = 384
LM = 512
OUT = 1024
NTOK = WORK * TOK


def dot(a, b, da=1, db=0):
    return lax.dot_general(a, b, (((da,), (db,)), ((), ())), preferred_element_type=F32)


def iota(shape, axis):
    return lax.broadcasted_iota(jnp.int32, shape, axis)


def turn(v, k, n):
    return lax.rem(v + (k % n), n)


def add_into(target, *others):
    def body(i, carry):
        total = target[i].astype(F32)
        for o in others:
            total = total + o[i].astype(F32)
        target[i] = total.astype(BF)
        return carry

    lax.fori_loop(0, target.shape[0], body, 0)


class Half:
    def __init__(self, kind, h, y, x, c, t):
        self.kind, self.h, self.y, self.x, self.c, self.t = kind, h, y, x, c, t
        self.q = x if h == 0 else y
        self.r = y if h == 0 else x

    def dev(self, y, x, c):
        return (y * 8 + x * 2 + c, self.t)

    def first(self, k):
        if self.h == 0:
            return self.dev(self.y, turn(self.x, k, 4), self.c)
        return self.dev(turn(self.y, k, 4), self.x, self.c)

    def second(self, k):
        if self.h == 0:
            return self.dev(turn(self.y, k, 4), self.x, self.c)
        return self.dev(self.y, turn(self.x, k, 4), self.c)

    def sibling(self):
        return self.dev(self.y, self.x, 1 - self.c)

    def cut(self, s):
        if self.kind == 2:
            start = 512 * self.h + (256 if s == 1 else 0)
            return pl.ds(0, 80), pl.ds(start, 512 if s is None else 256)
        start = 80 * self.h + (48 if s == 1 else 0)
        return pl.ds(start, {None: 80, 0: 48, 1: 32}[s]), pl.ds(0, HID)

    def at(self, buf, y, x, c, s):
        rows, cols = self.cut(s)
        if self.kind == 2:
            return buf.at[y, x, c, rows, cols]
        return buf.at[x, c, y, rows, cols]

    def block(self, buf, k, s=None):
        p = turn(self.q, k, 4)
        if self.h == 0:
            return self.at(buf, self.y, p, self.c, s)
        return self.at(buf, p, self.x, self.c, s)

    def group(self, buf, k, s=None, other=False):
        p = turn(self.r, k, 4)
        c = 1 - self.c if other else self.c
        if self.h == 0:
            return self.at(buf, p, slice(None), c, s)
        return self.at(buf, slice(None), p, c, s)


class Mail:
    def __init__(self, send, recv):
        self.s, self.r, self.started = send, recv, []

    def make(self, src, dst, i, device):
        return pltpu.make_async_remote_copy(
            src_ref=src,
            dst_ref=dst,
            send_sem=self.s.at[i],
            recv_sem=self.r.at[i],
            device_id=device,
            device_id_type=MESH,
        )

    def send(self, src, dst, i, device):
        copy = self.make(src, dst, i, device)
        copy.start()
        self.started.append(copy)

    def wait(self, dst, i, device):
        self.make(dst, dst, i, device).wait_recv()

    def finish(self):
        for copy in self.started:
            copy.wait_send()
        self.started = []


def plane_gather(hf, buf, mail):
    def send(ref, i, device):
        mail.send(ref, ref, i, device)

    def wait(ref, i):
        mail.wait(ref, i, hf.sibling())

    send(hf.block(buf, 0), 0, hf.first(1))
    send(hf.block(buf, 0), 1, hf.first(-1))
    yield
    wait(hf.block(buf, -1), 0)
    send(hf.block(buf, -1, 0), 2, hf.first(1))
    wait(hf.block(buf, 1), 1)
    send(hf.block(buf, 1, 1), 3, hf.first(-1))
    yield
    wait(hf.block(buf, 2, 0), 2)
    wait(hf.block(buf, 2, 1), 3)
    send(hf.group(buf, 0), 4, hf.second(1))
    send(hf.group(buf, 0), 5, hf.second(-1))
    send(hf.group(buf, 0), 6, hf.sibling())
    yield
    wait(hf.group(buf, -1), 4)
    send(hf.group(buf, -1, 0), 7, hf.second(1))
    send(hf.group(buf, -1), 8, hf.sibling())
    wait(hf.group(buf, 1), 5)
    send(hf.group(buf, 1, 1), 9, hf.second(-1))
    send(hf.group(buf, 1), 10, hf.sibling())
    yield
    wait(hf.group(buf, 2, 0), 7)
    wait(hf.group(buf, 2, 1), 9)
    send(hf.group(buf, 2), 11, hf.sibling())
    yield
    for k, i in ((0, 6), (-1, 8), (1, 10), (2, 11)):
        wait(hf.group(buf, k, None, True), i)
    yield


def plane_scatter(hf, buf, room, mail, put):
    cores, sub0, sub1, full, last0, last1, last = room

    def wait(ref, i):
        mail.wait(ref, i, hf.sibling())

    for n, k in enumerate((2, 1, -1, 0)):
        mail.send(hf.group(buf, k, None, True), cores.at[n], n, hf.sibling())
    yield
    wait(cores.at[0], 0)
    add_into(hf.group(buf, 2), cores.at[0])
    mail.send(hf.group(buf, 2, 0), sub0, 4, hf.second(1))
    mail.send(hf.group(buf, 2, 1), sub1, 5, hf.second(-1))
    wait(cores.at[1], 1)
    add_into(hf.group(buf, 1), cores.at[1])
    wait(cores.at[2], 2)
    add_into(hf.group(buf, -1), cores.at[2])
    yield
    wait(sub0, 4)
    add_into(hf.group(buf, 1, 0), sub0)
    mail.send(hf.group(buf, 1), full.at[0], 6, hf.second(1))
    wait(sub1, 5)
    add_into(hf.group(buf, -1, 1), sub1)
    mail.send(hf.group(buf, -1), full.at[1], 7, hf.second(-1))
    wait(cores.at[3], 3)
    add_into(hf.group(buf, 0), cores.at[3])
    yield
    wait(full.at[0], 6)
    wait(full.at[1], 7)
    add_into(hf.group(buf, 0), full.at[0], full.at[1])
    mail.send(hf.block(buf, 2, 0), last0, 8, hf.first(1))
    mail.send(hf.block(buf, 2, 1), last1, 9, hf.first(-1))
    yield
    wait(last0, 8)
    near = hf.block(buf, 1, 0)
    near[...] = (near[...].astype(F32) + last0[...].astype(F32)).astype(BF)
    mail.send(hf.block(buf, 1), last.at[0], 10, hf.first(1))
    wait(last1, 9)
    near = hf.block(buf, -1, 1)
    near[...] = (near[...].astype(F32) + last1[...].astype(F32)).astype(BF)
    mail.send(hf.block(buf, -1), last.at[1], 11, hf.first(-1))
    yield
    wait(last.at[0], 10)
    wait(last.at[1], 11)
    put(
        hf.block(buf, 0)[...].astype(F32)
        + last[0].astype(F32)
        + last[1].astype(F32)
    )
    yield


def ring_gather(dp, t, buf, cuts, mail):
    up, down = (dp, turn(t, 1, NZ)), (dp, turn(t, -1, NZ))

    def view(k, cut):
        return buf.at[turn(t, k, NZ), cut, :]

    def send(k, cut, i, device):
        mail.send(view(k, cut), view(k, cut), i, device)

    def wait(k, cut, i):
        mail.wait(view(k, cut), i, up)

    for n, (whole, _, _) in enumerate(cuts):
        send(0, whole, (n, 0), up)
        send(0, whole, (n, 1), down)
    yield (0,)
    for k in (1, 2):
        for n, (whole, _, _) in enumerate(cuts):
            wait(-k, whole, (n, 2 * k - 2))
            send(-k, whole, (n, 2 * k), up)
            wait(k, whole, (n, 2 * k - 1))
            send(k, whole, (n, 2 * k + 1), down)
        yield (-k, k)
    for n, (whole, one, two) in enumerate(cuts):
        wait(-3, whole, (n, 4))
        send(-3, one, (n, 6), up)
        wait(3, whole, (n, 5))
        send(3, two, (n, 7), down)
    yield (-3, 3)
    for n, (_, one, two) in enumerate(cuts):
        wait(4, one, (n, 6))
        wait(4, two, (n, 7))
    yield (4,)


def ring_scatter(dp, t, buf, room, mail, put):
    up, down = (dp, turn(t, 1, NZ)), (dp, turn(t, -1, NZ))
    half = HID // 2
    low, high = pl.ds(0, half), pl.ds(half, half)

    def view(k, cut):
        return buf.at[turn(t, k, NZ), cut, :]

    def plus(k, cut, other):
        mine = view(k, cut)
        mine[...] = (mine[...].astype(F32) + other[...].astype(F32)).astype(BF)

    mail.send(view(4, low), room.at[0, low, :], 0, up)
    mail.send(view(4, high), room.at[1, high, :], 1, down)
    yield
    every = pl.ds(0, HID)
    for n, k in enumerate((3, 2, 1)):
        a, b = (low, high) if n == 0 else (every, every)
        mail.wait(room.at[2 * n, a, :], 2 * n, up)
        plus(k, a, room.at[2 * n, a, :])
        mail.send(view(k, every), room.at[2 * n + 2], 2 * n + 2, up)
        mail.wait(room.at[2 * n + 1, b, :], 2 * n + 1, up)
        plus(-k, b, room.at[2 * n + 1, b, :])
        mail.send(view(-k, every), room.at[2 * n + 3], 2 * n + 3, down)
        yield
    mail.wait(room.at[6], 6, up)
    mail.wait(room.at[7], 7, up)
    put(view(0, every)[...].astype(F32) + room[6].astype(F32) + room[7].astype(F32))
    yield


def body(
    win, gain, fc1, fc2, text, lmg,
    lm_out, g1_out, g2_out,
    sq, xn, st1, rv1, st2, rv2, xs, f1, f2, up_rows, place,
    acc, slope, hid, hb, hb_room, dz, mixed, p1, p2,
    a_cores, a_sub0, a_sub1, a_full, a_last0, a_last1, a_last,
    b_cores, b_sub, b_full, b_lasts, b_last,
    sq_s, sq_r, hop_s, hop_r, ag_s, ag_r, zx_s, zx_r, zh_s, zh_r, zb_s, zb_r, rs_s, rs_r,
):
    dp = lax.axis_index("dp")
    t = lax.axis_index("tensor")
    y, x, c = lax.div(dp, 8), lax.rem(lax.div(dp, 2), 4), lax.rem(dp, 2)

    barrier = pltpu.get_barrier_semaphore()

    def greet(k, carry):
        pl.semaphore_signal(
            barrier, inc=1, device_id=(lax.rem(dp + k, NDP), t), device_id_type=MESH
        )
        return carry

    lax.fori_loop(1, NDP, greet, 0)

    def greet_z(k, carry):
        pl.semaphore_signal(
            barrier, inc=1, device_id=(dp, lax.rem(t + k, NZ)), device_id_type=MESH
        )
        return carry

    lax.fori_loop(1, NZ, greet_z, 0)

    f2[y, x, c] = fc2[...]
    f1[x, c, y] = fc1[...]

    rows = SRC * TOK
    seg = iota((rows, FEAT), 1) // 160
    value = win[:, :FEAT].astype(F32)
    square = value * value
    lane = iota((rows, 128), 1)
    table = jnp.zeros((rows, 128), F32)
    for p in range(4):
        part = jnp.sum(jnp.where(seg == p, square, 0.0), axis=1, keepdims=True)
        table = jnp.where(lane == p, part, table)
    sq[t] = table.T[:8]

    pl.semaphore_wait(barrier, NDP - 1 + NZ - 1)

    def sq_copy(k, j):
        return pltpu.make_async_remote_copy(
            src_ref=sq.at[t], dst_ref=sq.at[t], send_sem=sq_s.at[k], recv_sem=sq_r.at[t],
            device_id=(dp, j), device_id_type=MESH,
        )

    def sq_wait(k):
        j = lax.rem(t + k, NZ)
        pltpu.make_async_remote_copy(
            src_ref=sq.at[j], dst_ref=sq.at[j], send_sem=sq_s.at[k], recv_sem=sq_r.at[j],
            device_id=(dp, j), device_id_type=MESH,
        ).wait_recv()

    for k in range(1, NZ):
        sq_copy(k, lax.rem(t + k, NZ)).start()

    halves = [Half(kind, h, y, x, c, t) for kind in (2, 1) for h in (0, 1)]
    ag_mail = [Mail(ag_s.at[n], ag_r.at[n]) for n in range(4)]
    gathers = [
        plane_gather(hf, f2 if hf.kind == 2 else f1, m) for hf, m in zip(halves, ag_mail)
    ]

    def step(generators):
        for g in generators:
            next(g)

    step(gathers)

    for k in range(1, NZ):
        sq_wait(k)
    total = jnp.sum(sq[...], axis=0)
    scale = lax.rsqrt(total * (1.0 / DM) + 1e-06)
    scale = jnp.concatenate([scale] * 16, axis=0).T
    spread = jnp.where(
        seg == 0,
        scale[:, 0:1],
        jnp.where(seg == 1, scale[:, 1:2], jnp.where(seg == 2, scale[:, 2:3], scale[:, 3:4])),
    )
    xn[:, :FEAT] = (win[:, :FEAT].astype(F32) * spread * gain[pl.ds(t, 1), :]).astype(BF)
    xn[:, FEAT:] = win[:, FEAT:]

    def facts(ref_rows):
        return ref_rows.astype(F32).T

    def pick(count, number, key, ok):
        n = key.shape[1]
        r, q = iota((count, n), 0), iota((count, n), 1)
        hit = (lax.div(r, TOK) == key) & (lax.rem(r, TOK) == lax.rem(q, TOK)) & (ok > 0.5)
        return jnp.where(hit, 1.0, 0.0).astype(BF)

    def hop_copy(n, src, dst, k):
        j = lax.rem(dp + k, NDP)
        return pltpu.make_async_remote_copy(
            src_ref=src.at[j], dst_ref=dst.at[dp], send_sem=hop_s.at[n, k], recv_sem=hop_r.at[n, dp],
            device_id=(j, t), device_id_type=MESH,
        )

    def hop_send(n, src, dst):
        def one(k, carry):
            hop_copy(n, src, dst, k).start()
            return carry

        lax.fori_loop(1, NDP, one, 0)
        dst[dp] = src[dp]

    def hop_wait(n, src, dst):
        def one(k, carry):
            j = lax.rem(dp + k, NDP)
            pltpu.make_async_remote_copy(
                src_ref=src.at[j], dst_ref=dst.at[j], send_sem=hop_s.at[n, k], recv_sem=hop_r.at[n, j],
                device_id=(j, t), device_id_type=MESH,
            ).wait_recv()
            return carry

        lax.fori_loop(1, NDP, one, 0)

    def hop_done(n, src, dst):
        def one(k, carry):
            hop_copy(n, src, dst, k).wait_send()
            return carry

        lax.fori_loop(1, NDP, one, 0)

    m = facts(xn[:, FEAT:])
    chosen = pick(NDP * TOK, None, m[3:4].astype(jnp.int32), m[0:1])
    st1[...] = dot(chosen, xn[...]).astype(BF).reshape(NDP, TOK, WIDE)
    hop_send(0, st1, rv1)
    step(gathers)

    hop_wait(0, st1, rv1)
    m = facts(rv1[:, :, FEAT:].reshape(NDP * TOK, 128))
    owner = lax.div(m[1:2].astype(jnp.int32), LM // 128)
    chosen = pick(NDP * TOK, None, owner, m[0:1])
    st2[...] = dot(chosen, rv1[...].reshape(NDP * TOK, WIDE)).astype(BF).reshape(NDP, TOK, WIDE)
    hop_send(1, st2, rv2)
    step(gathers)

    hop_wait(1, st2, rv2)
    m = facts(rv2[:, :, FEAT:].reshape(NDP * TOK, 128))
    n = NDP * TOK
    before = (lax.div(iota((n, n), 0), TOK) < lax.div(iota((n, n), 1), TOK)) & (
        lax.rem(iota((n, n), 0), TOK) == 0
    )
    live8 = jnp.broadcast_to(m[0:1], (16, n)).astype(BF)
    rank = dot(live8, jnp.where(before, 1.0, 0.0).astype(BF))[0:1]
    chosen = pick(NTOK, None, (rank + 0.5).astype(jnp.int32), m[0:1])
    work = dot(chosen, rv2[...].reshape(n, WIDE))
    xs[t] = work[:, :FEAT].astype(BF)

    zx_mail = Mail(zx_s, zx_r)
    zx = ring_gather(
        dp, t, xs,
        [(pl.ds(0, 128), pl.ds(0, 64), pl.ds(64, 64)), (pl.ds(128, 128), pl.ds(128, 64), pl.ds(192, 64))],
        zx_mail,
    )
    x_order = list(next(zx))

    base = dp * LM
    mcol = work[:, FEAT:]
    mrow = mcol.T
    tok_col = (mcol[:, 1:2] * 128.0 + mcol[:, 2:3] + 0.5).astype(jnp.int32) - base
    tok_row = (mrow[1:2] * 128.0 + mrow[2:3] + 0.5).astype(jnp.int32) - base
    fetch = jnp.where(iota((NTOK, LM), 1) == tok_col, 1.0, 0.0).astype(BF)
    place[...] = jnp.where(iota((LM, NTOK), 0) == tok_row, 1.0, 0.0).astype(BF)
    up_rows[...] = dot(fetch, lmg[...]).astype(BF)

    step(gathers)
    x_order += list(next(zx))
    step(gathers)
    x_order += list(next(zx))
    step(gathers)

    def second_rows(k):
        two = lax.rem(k, 2) * 2
        return f2[lax.div(k, 2), pl.ds(two, 2)].reshape(HID, OUT)

    def back(k, carry):
        hb[k] = dot(second_rows(k), up_rows[...], 1, 1).astype(BF)
        return carry

    lax.fori_loop(0, NZ, back, 0)

    zb_mail = Mail(zb_s, zb_r)

    def put_back(total):
        acc[:HID, :] = total

    zb = ring_scatter(dp, t, hb, hb_room, zb_mail, put_back)

    def first_part(k):
        j = turn(t, k, NZ)
        w = f1[lax.div(j, 2), lax.rem(j, 2)].reshape(FEAT, HID)
        return dot(xs[j], w)

    z1 = None
    for k in x_order:
        term = first_part(k)
        z1 = term if z1 is None else z1 + term
    for order in zx:
        for k in order:
            z1 = z1 + first_part(k)
    next(zb)
    z1 = jnp.concatenate([z1, jnp.zeros((NTOK, HPAD - HID), F32)], axis=1).T[:HID]
    cdf = 0.5 * (1.0 + lax.erf(z1 * 0.7071067811865476))
    hid[t] = (z1 * cdf).astype(BF)
    slope[...] = cdf + z1 * (jnp.exp(-0.5 * z1 * z1) * 0.3989422804014327)

    zh_mail = Mail(zh_s, zh_r)
    zh = ring_gather(dp, t, hid, [(pl.ds(0, 320), pl.ds(0, 160), pl.ds(160, 160))], zh_mail)
    mixed[...] = jnp.zeros_like(mixed)

    def use_hidden(k):
        j = turn(t, k, NZ)
        h = hid[j]
        mixed[...] += dot(h, second_rows(j), 0, 0)
        two = lax.rem(j, 2) * 2
        p2[lax.div(j, 2), pl.ds(two, 2)] = dot(h, up_rows[...]).astype(BF).reshape(2, 2, 80, OUT)

    for order in zh:
        for k in order:
            use_hidden(k)
        next(zb, None)

    rs_mail = [Mail(rs_s.at[n], rs_r.at[n]) for n in range(4)]

    def put2(h):
        def put(total):
            g2_out[:, 512 * h : 512 * h + 512] = total

        return put

    def put1(h):
        def put(total):
            g1_out[80 * h : 80 * h + 80, :] = total

        return put

    scatters = []
    for n, hf in enumerate(halves):
        h = hf.h
        if hf.kind == 2:
            room = (b_cores.at[h], b_sub.at[h, 0], b_sub.at[h, 1], b_full.at[h],
                    b_lasts.at[h, 0], b_lasts.at[h, 1], b_last.at[h])
            scatters.append(plane_scatter(hf, p2, room, rs_mail[n], put2(h)))
        else:
            room = (a_cores.at[h], a_sub0.at[h], a_sub1.at[h], a_full.at[h],
                    a_last0.at[h], a_last1.at[h], a_last.at[h])
            scatters.append(plane_scatter(hf, p1, room, rs_mail[n], put1(h)))
    step(scatters[:2])

    for _ in zb:
        pass
    dz_t = acc[:HID, :] * slope[...]
    dz[...] = jnp.concatenate([dz_t, jnp.zeros((HPAD - HID, NTOK), F32)], axis=0).T.astype(BF)

    def grad1(k, carry):
        term = dot(xs[k], dz[:, :HID], 0, 0).astype(BF)
        p1[lax.div(k, 2), lax.rem(k, 2)] = term.reshape(4, 160, HID)
        return carry

    lax.fori_loop(0, NZ, grad1, 0)
    step(scatters[2:])
    step(scatters[:2])

    merged = mixed[...].astype(BF)
    covered = jnp.max(place[...].astype(F32), axis=1, keepdims=True) > 0.5
    lm_out[...] = jnp.where(covered, dot(place[...], merged), text[...].astype(F32)).astype(BF)

    for _ in range(4):
        step(scatters[2:])
        step(scatters[:2])
    step(scatters[2:])

    for k in range(1, NZ):
        sq_copy(k, lax.rem(t + k, NZ)).wait_send()
    hop_done(0, st1, rv1)
    hop_done(1, st2, rv2)
    for m in ag_mail + rs_mail + [zx_mail, zh_mail, zb_mail]:
        m.finish()


def per_device(patches, gain, window_dest, window_pos, fc1, fc2, text_embeds, lm_grad):
    rows = SRC * TOK
    live = window_pos >= 0
    pos = jnp.where(live, window_pos, 0)[:, None] + jnp.arange(TOK, dtype=jnp.int32)[None, :]
    lane = jnp.arange(128, dtype=jnp.int32)[None, None, :]
    pos = pos[:, :, None]
    facts = jnp.where(
        lane == 0,
        live[:, None, None].astype(jnp.int32),
        jnp.where(
            lane == 1,
            pos // 128,
            jnp.where(lane == 2, pos % 128, jnp.where(lane == 3, window_dest[:, None, None], 0)),
        ),
    )
    win = jnp.concatenate(
        [patches.reshape(rows, FEAT), facts.astype(BF).reshape(rows, 128)], axis=1
    )
    gains = jnp.tile(gain.reshape(NZ, 160), (1, 4))
    vm = pl.BlockSpec(memory_space=pltpu.VMEM)
    V = pltpu.VMEM
    D = pltpu.SemaphoreType.DMA
    scratch = [
        V((NZ, 8, rows), F32),
        V((rows, WIDE), BF),
        V((NDP, TOK, WIDE), BF),
        V((NDP, TOK, WIDE), BF),
        V((NDP, TOK, WIDE), BF),
        V((NDP, TOK, WIDE), BF),
        V((NZ, NTOK, FEAT), BF),
        V((4, 2, 4, 160, HID), BF),
        V((4, 4, 2, 80, OUT), BF),
        V((NTOK, OUT), BF),
        V((LM, NTOK), BF),
        V((HID, NTOK), F32),
        V((HID, NTOK), F32),
        V((NZ, HID, NTOK), BF),
        V((NZ, HID, NTOK), BF),
        V((8, HID, NTOK), BF),
        V((NTOK, HPAD), BF),
        V((NTOK, OUT), F32),
        V((4, 2, 4, 160, HID), BF),
        V((4, 4, 2, 80, OUT), BF),
        V((2, 4, 4, 80, HID), BF),
        V((2, 4, 48, HID), BF),
        V((2, 4, 32, HID), BF),
        V((2, 2, 4, 80, HID), BF),
        V((2, 48, HID), BF),
        V((2, 32, HID), BF),
        V((2, 2, 80, HID), BF),
        V((2, 4, 4, 80, 512), BF),
        V((2, 2, 4, 80, 256), BF),
        V((2, 2, 4, 80, 512), BF),
        V((2, 2, 80, 256), BF),
        V((2, 2, 80, 512), BF),
        D((NZ,)), D((NZ,)),
        D((2, NDP)), D((2, NDP)),
        D((4, 12)), D((4, 12)),
        D((2, 8)), D((2, 8)),
        D((1, 8)), D((1, 8)),
        D((8,)), D((8,)),
        D((4, 12)), D((4, 12)),
    ]
    return pl.pallas_call(
        body,
        out_shape=(
            jax.ShapeDtypeStruct((LM, OUT), BF),
            jax.ShapeDtypeStruct((160, HID), F32),
            jax.ShapeDtypeStruct((80, OUT), F32),
        ),
        in_specs=[vm] * 6,
        out_specs=(vm, vm, vm),
        scratch_shapes=scratch,
        compiler_params=pltpu.CompilerParams(
            collective_id=0, has_side_effects=True, vmem_limit_bytes=60 * 1024 * 1024
        ),
        cost_estimate=pl.CostEstimate(
            flops=6_000_000_000, bytes_accessed=8_000_000, transcendentals=300_000
        ),
    )(win, gains, fc1, fc2, text_embeds, lm_grad)


def solution(mesh):
    both = P("dp", "tensor")
    return jax.shard_map(
        per_device,
        mesh=mesh,
        in_specs=(both, P(), P("dp"), P("dp"), both, both, both, both),
        out_specs=(both, both, both),
        check_vma=False,
    )
```

time: 507 us -> 152 us (0.30); the launches traced: 500 us -> 150 us
  waiting for transfers between devices: 343 us -> 0 us
  Pallas kernels: 0 us -> 139 us
  local copies, waits for them, and re-layouts: 44.2 us -> 7.84 us
  starting transfers between devices: 34.2 us -> 0 us
  other arithmetic: 34.1 us -> 3.23 us
  matrix products: 30 us -> 0 us
  between operations: 14.7 us -> 0.7 us
    reduce_scatter x3 -> x0, waiting for transfers between devices: 169 us -> none  [the longest x1 91.5 us: per_device(): lax.psum_scatter(lax.dot_general(columns, slope, (((0,), (0,)), ((), ()))...]
    pallas_call x0 -> x1, Pallas kernels: none -> 139 us  [per_device(): pl.pallas_call(body, out_shape=(jax.ShapeDtypeStruct((LM, OUT), BF), jax....]
    all_gather x4 -> x0, waiting for transfers between devices: 122 us -> none  [the longest x1 49.7 us: per_device(): full = lax.all_gather(work, 'tensor', axis=2, tiled=True)]
    all_to_all x5 -> x0, waiting for transfers between devices: 49.8 us -> none  [the longest x1 17.5 us: per_device(): lax.all_to_all(returned, 'dp', split_axis=0, concat_axis=0, tiled=True)]
    all_to_all x5 -> x0, starting transfers between devices: 33.6 us -> none  [the longest x1 7.71 us: per_device(): lax.all_to_all(parcel, 'dp', split_axis=0, concat_axis=0, tiled=True)]
    dot_general x7 -> x0, matrix products: 30 us -> none  [the longest x1 5.74 us: per_device(): jnp.dot(columns, lax.all_gather(fc1, 'dp', axis=0, tiled=True), preferred...]
    reshape x8 -> x1, local copies, waits for them, and re-layouts: 15.2 us -> 1.09 us  [per_device(): patches.reshape(rows, FEAT)]
    all_to_all x2 -> x0, other arithmetic: 8.05 us -> none  [the longest x1 7.38 us: per_device(): lax.all_to_all(parcel, 'dp', split_axis=0, concat_axis=0, tiled=True)]
  transfers between devices with their start and end apart: 12 -> 0, of which waited for: 11 -> 0; matrix products, arithmetic and copies ran while one was open for 19% -> 0% of each run, Pallas kernels for 0% -> 0%
where the time goes in v1:
time: 152 us; the launch traced here: 150 us
  Pallas kernels  139 us (91%)
  local copies, waits for them, and re-layouts  7.84 us (5%)
  other arithmetic  3.23 us (2%)
    pallas_call x1, Pallas kernels, per_device(): pl.pallas_call(body, out_shape=(jax.ShapeDtypeStruct((LM, OUT), BF), jax....  139 us
    unnamed x8, local copies, waits for them, and re-layouts  5.05 us

profile of v1, /device:TPU:2, one launch (start us, length us, event | category | flops | bytes accessed | tf_op | source)
XLA Modules:
  0.0 150.3 jit_solution(9573481252916562129)
XLA Ops:
  0.6 0.7 compare_select_fusion
  1.3 0.7 compare_convert_fusion
  2.0 0.8 tile.10
  2.7 0.7 broadcast_select_fusion
  3.5 0.1 broadcast_in_dim.91
  3.5 0.1 broadcast_in_dim.92
  3.6 0.1 iota_add_fusion
  3.7 0.1 add.43
  3.8 0.7 tile.12.gain
  4.5 0.2 fusion.2
  4.7 1.3 copy.12
  6.0 1.1 reshape.154
  7.1 0.9 pad_maximum_fusion.win
  8.0 138.5 %shard_map.103 = (bf16[512,1024]{1,0:T(8,128)(2,1)}, f32[160,320]{1,0:T(8,128)}, f32[80,1024]{1,0:T(8,128)}) custom-call(bf16[384,768]{1,0:T(8,128)(2,1)} %pad_maximum_fusion.win, f32[8,640]{1,0:T(8,128)} %tile.12.gain, bf16[160,320]{1,0:T(8,128)(2,1)} %fc1.1, bf16[80,1024]{1,0:T(8,128)(2,1)} %fc2.1, bf16[512,1024]{1,0:T(8,128)(2,1)} %text.1, ...), custom_call_target="tpu_custom_call" | custom-call | flops 6000000000 | bytes 8000000 | tf_op jit(solution)/shard_map/pallas_call | solution.py:634
  146.5 0.0 copy-start.1
  146.5 0.0 copy-start
  146.5 2.3 %copy.16 = bf16[512,1024]{1,0:T(8,128)(2,1)} copy(bf16[512,1024]{1,0:T(8,128)(2,1)} %get-tuple-element.10) | data formatting | bytes 2097152
  148.9 0.0 copy-done.1
  148.9 0.7 copy.17
  149.6 0.0 copy-done
  149.6 0.7 copy.18
  (5 shorter events, 0.0 us)
Async XLA Ops:
  146.5 2.3 %copy-start.1 = (f32[160,320]{1,0:T(8,128)S(1)}, f32[160,320]{1,0:T(8,128)}, u32[]{:S(2)}) copy-start(f32[160,320]{1,0:T(8,128)} %get-tuple-element.11) | copy-start | bytes 614404
  146.5 3.0 %copy-start = (f32[80,1024]{1,0:T(8,128)S(1)}, f32[80,1024]{1,0:T(8,128)}, u32[]{:S(2)}) copy-start(f32[80,1024]{1,0:T(8,128)} %get-tuple-element.12) | copy-start | bytes 983044

commit v2 on v1

v2 whole, which is shorter than its diff:
```python
import functools

import jax
import jax.numpy as jnp
from jax import lax
from jax.experimental import pallas as pl
from jax.experimental.pallas import tpu as pltpu
from jax.sharding import PartitionSpec as P

MESH = pl.DeviceIdType.MESH
BF = jnp.bfloat16
F32 = jnp.float32
DM = 1280
NDP = 32
NZ = 8
SRC = 24
WORK = 16
TOK = 16
FEAT = 640
WIN = 64
HID = 320
HPAD = 384
LM = 512
OUT = 1024
NTOK = WORK * TOK


def dot(a, b, da=1, db=0):
    return lax.dot_general(a, b, (((da,), (db,)), ((), ())), preferred_element_type=F32)


def iota(shape, axis):
    return lax.broadcasted_iota(jnp.int32, shape, axis)


def turn(v, k, n):
    return lax.rem(v + (k % n), n)


class Half:
    def __init__(self, kind, h, y, x, c, t):
        self.kind, self.h, self.y, self.x, self.c, self.t = kind, h, y, x, c, t
        self.q = x if h == 0 else y
        self.r = y if h == 0 else x

    def dev(self, y, x, c):
        return (y * 8 + x * 2 + c, self.t)

    def first(self, k):
        if self.h == 0:
            return self.dev(self.y, turn(self.x, k, 4), self.c)
        return self.dev(turn(self.y, k, 4), self.x, self.c)

    def second(self, k):
        if self.h == 0:
            return self.dev(turn(self.y, k, 4), self.x, self.c)
        return self.dev(self.y, turn(self.x, k, 4), self.c)

    def sibling(self):
        return self.dev(self.y, self.x, 1 - self.c)

    def cut(self, s):
        if self.kind == 2:
            start = 512 * self.h + (256 if s == 1 else 0)
            return pl.ds(0, 80), pl.ds(start, 512 if s is None else 256)
        start = 80 * self.h + (48 if s == 1 else 0)
        return pl.ds(start, {None: 80, 0: 48, 1: 32}[s]), pl.ds(0, HID)

    def at(self, buf, y, x, c, s):
        rows, cols = self.cut(s)
        if self.kind == 2:
            return buf.at[y, x, c, rows, cols]
        return buf.at[x, c, y, rows, cols]

    def block(self, buf, k, s=None):
        p = turn(self.q, k, 4)
        if self.h == 0:
            return self.at(buf, self.y, p, self.c, s)
        return self.at(buf, p, self.x, self.c, s)

    def cell(self, buf, g, b, s=None):
        p, q = turn(self.r, g, 4), turn(self.q, b, 4)
        if self.h == 0:
            return self.at(buf, p, q, self.c, s)
        return self.at(buf, q, p, self.c, s)

    def group(self, buf, k, s=None, other=False):
        p = turn(self.r, k, 4)
        c = 1 - self.c if other else self.c
        if self.h == 0:
            return self.at(buf, p, slice(None), c, s)
        return self.at(buf, slice(None), p, c, s)


class Mail:
    def __init__(self, send, recv):
        self.s, self.r, self.started = send, recv, []

    def make(self, src, dst, i, device):
        return pltpu.make_async_remote_copy(
            src_ref=src,
            dst_ref=dst,
            send_sem=self.s.at[i],
            recv_sem=self.r.at[i],
            device_id=device,
            device_id_type=MESH,
        )

    def send(self, src, dst, i, device):
        copy = self.make(src, dst, i, device)
        copy.start()
        self.started.append(copy)

    def wait(self, dst, i, device):
        self.make(dst, dst, i, device).wait_recv()

    def finish(self):
        for copy in self.started:
            copy.wait_send()
        self.started = []


def plane_gather(hf, buf, mail):
    def send(ref, i, device):
        mail.send(ref, ref, i, device)

    def wait(ref, i):
        mail.wait(ref, i, hf.sibling())

    send(hf.block(buf, 0), 0, hf.first(1))
    send(hf.block(buf, 0), 1, hf.first(-1))
    yield
    wait(hf.block(buf, -1), 0)
    send(hf.block(buf, -1, 0), 2, hf.first(1))
    wait(hf.block(buf, 1), 1)
    send(hf.block(buf, 1, 1), 3, hf.first(-1))
    yield
    wait(hf.block(buf, 2, 0), 2)
    wait(hf.block(buf, 2, 1), 3)
    send(hf.group(buf, 0), 4, hf.second(1))
    send(hf.group(buf, 0), 5, hf.second(-1))
    send(hf.group(buf, 0), 6, hf.sibling())
    yield
    wait(hf.group(buf, -1), 4)
    send(hf.group(buf, -1, 0), 7, hf.second(1))
    send(hf.group(buf, -1), 8, hf.sibling())
    wait(hf.group(buf, 1), 5)
    send(hf.group(buf, 1, 1), 9, hf.second(-1))
    send(hf.group(buf, 1), 10, hf.sibling())
    yield
    wait(hf.group(buf, 2, 0), 7)
    wait(hf.group(buf, 2, 1), 9)
    send(hf.group(buf, 2), 11, hf.sibling())
    yield
    for k, i in ((0, 6), (-1, 8), (1, 10), (2, 11)):
        wait(hf.group(buf, k, None, True), i)
    yield


def ring_sums(hf, buf, room, mail, put):
    sub0, sub1, full, last0, last1, last = room
    order = (2, 1, -1, 0)

    def wait(ref, i):
        mail.wait(ref, i, hf.sibling())

    def plus(mine, *others):
        total = mine[...].astype(F32)
        for o in others:
            total = total + o[...].astype(F32)
        mine[...] = total.astype(BF)

    for n, b in enumerate(order):
        mail.send(hf.cell(buf, 2, b, 0), sub0.at[n], n, hf.second(1))
        mail.send(hf.cell(buf, 2, b, 1), sub1.at[n], 4 + n, hf.second(-1))
    yield
    for n, b in enumerate(order):
        wait(sub0.at[n], n)
        plus(hf.cell(buf, 1, b, 0), sub0.at[n])
        mail.send(hf.cell(buf, 1, b), full.at[0, n], 8 + n, hf.second(1))
        wait(sub1.at[n], 4 + n)
        plus(hf.cell(buf, -1, b, 1), sub1.at[n])
        mail.send(hf.cell(buf, -1, b), full.at[1, n], 12 + n, hf.second(-1))
    yield
    for n in (0, 1, 2):
        wait(full.at[0, n], 8 + n)
        wait(full.at[1, n], 12 + n)
        plus(hf.cell(buf, 0, order[n]), full.at[0, n], full.at[1, n])
        if n == 0:
            mail.send(hf.block(buf, 2, 0), last0, 16, hf.first(1))
            mail.send(hf.block(buf, 2, 1), last1, 17, hf.first(-1))
    yield
    wait(last0, 16)
    plus(hf.block(buf, 1, 0), last0)
    mail.send(hf.block(buf, 1), last.at[0], 18, hf.first(1))
    wait(last1, 17)
    plus(hf.block(buf, -1, 1), last1)
    mail.send(hf.block(buf, -1), last.at[1], 19, hf.first(-1))
    yield
    wait(full.at[0, 3], 11)
    wait(full.at[1, 3], 15)
    wait(last.at[0], 18)
    wait(last.at[1], 19)
    total = hf.block(buf, 0)[...].astype(F32)
    for part in (full[0, 3], full[1, 3], last[0], last[1]):
        total = total + part.astype(F32)
    put(total)
    yield


def ring_gather(dp, t, buf, cuts, mail):
    up, down = (dp, turn(t, 1, NZ)), (dp, turn(t, -1, NZ))

    def view(k, cut):
        return buf.at[(turn(t, k, NZ),) + cut]

    def send(k, cut, i, device):
        mail.send(view(k, cut), view(k, cut), i, device)

    def wait(k, cut, i):
        mail.wait(view(k, cut), i, up)

    whole, one, two = cuts
    send(0, whole, 0, up)
    send(0, whole, 1, down)
    yield (0,)
    for k in (1, 2):
        wait(-k, whole, 2 * k - 2)
        send(-k, whole, 2 * k, up)
        wait(k, whole, 2 * k - 1)
        send(k, whole, 2 * k + 1, down)
        yield (-k, k)
    wait(-3, whole, 4)
    send(-3, one, 6, up)
    wait(3, whole, 5)
    send(3, two, 7, down)
    yield (-3, 3)
    wait(4, one, 6)
    wait(4, two, 7)
    yield (4,)


def ring_scatter(dp, t, buf, room, mail, put):
    up, down = (dp, turn(t, 1, NZ)), (dp, turn(t, -1, NZ))
    half = HID // 2
    low, high = pl.ds(0, half), pl.ds(half, half)

    def view(k, cut):
        return buf.at[turn(t, k, NZ), cut, :]

    def plus(k, cut, other):
        mine = view(k, cut)
        mine[...] = (mine[...].astype(F32) + other[...].astype(F32)).astype(BF)

    mail.send(view(4, low), room.at[0, low, :], 0, up)
    mail.send(view(4, high), room.at[1, high, :], 1, down)
    yield
    every = pl.ds(0, HID)
    for n, k in enumerate((3, 2, 1)):
        a, b = (low, high) if n == 0 else (every, every)
        mail.wait(room.at[2 * n, a, :], 2 * n, up)
        plus(k, a, room.at[2 * n, a, :])
        mail.send(view(k, every), room.at[2 * n + 2], 2 * n + 2, up)
        mail.wait(room.at[2 * n + 1, b, :], 2 * n + 1, up)
        plus(-k, b, room.at[2 * n + 1, b, :])
        mail.send(view(-k, every), room.at[2 * n + 3], 2 * n + 3, down)
        yield
    mail.wait(room.at[6], 6, up)
    mail.wait(room.at[7], 7, up)
    put(view(0, every)[...].astype(F32) + room[6].astype(F32) + room[7].astype(F32))
    yield


def body(
    patches_t, gain, dest, pos, fc1, fc2, text, lmg,
    lm_out, g1_out, g2_out,
    sq, meta, flat, st1, rv1, st2, rv2, xs, f1, f2, up_rows, place,
    acc, slope, hid, hb, hb_room, dz, mixed, p1, p2,
    a_cores, a_sub0, a_sub1, a_full, a_last0, a_last1, a_last,
    b_cores, b_sub, b_full, b_lasts, b_last,
    sq_s, sq_r, meta_s, meta_r, hop_s, hop_r, ag_s, ag_r, zx_s, zx_r, zh_s, zh_r, zb_s, zb_r,
    co_s, co_r, rs_s, rs_r,
):
    dp = lax.axis_index("dp")
    t = lax.axis_index("tensor")
    y, x, c = lax.div(dp, 8), lax.rem(lax.div(dp, 2), 4), lax.rem(dp, 2)
    sibling = (y * 8 + x * 2 + 1 - c, t)

    barrier = pltpu.get_barrier_semaphore()

    def greet(k, carry):
        pl.semaphore_signal(
            barrier, inc=1, device_id=(lax.rem(dp + k, NDP), t), device_id_type=MESH
        )
        return carry

    lax.fori_loop(1, NDP, greet, 0)

    def greet_z(k, carry):
        pl.semaphore_signal(
            barrier, inc=1, device_id=(dp, lax.rem(t + k, NZ)), device_id_type=MESH
        )
        return carry

    lax.fori_loop(1, NZ, greet_z, 0)

    r, q = iota((8, 128), 0), iota((8, 128), 1)
    table = jnp.full((8, 128), -1, jnp.int32)
    for s in range(SRC):
        table = jnp.where(q == s, jnp.where(r == 0, dest[s], pos[s]), table)
    meta[dp] = table

    value = patches_t[...].astype(F32)
    sq[t] = jnp.sum(value * value, axis=0, keepdims=True)
    f2[y, x, c] = fc2[...]
    f1[x, c, y] = fc1[...]

    pl.semaphore_wait(barrier, NDP - 1 + NZ - 1)

    def sq_copy(k, j, own):
        place_of = t if own else j
        return pltpu.make_async_remote_copy(
            src_ref=sq.at[place_of], dst_ref=sq.at[place_of], send_sem=sq_s.at[k], recv_sem=sq_r.at[place_of],
            device_id=(dp, j), device_id_type=MESH,
        )

    for k in range(1, NZ):
        sq_copy(k, lax.rem(t + k, NZ), True).start()

    def spread(copy):
        def start(k, carry):
            copy(k, lax.rem(dp + k, NDP), True).start()
            return carry

        def arrive(k, carry):
            copy(k, lax.rem(dp + k, NDP), False).wait_recv()
            return carry

        def sent(k, carry):
            copy(k, lax.rem(dp + k, NDP), True).wait_send()
            return carry

        return [functools.partial(lax.fori_loop, 1, NDP, f, 0) for f in (start, arrive, sent)]

    def meta_copy(k, j, own):
        place_of = dp if own else j
        return pltpu.make_async_remote_copy(
            src_ref=meta.at[place_of], dst_ref=meta.at[place_of], send_sem=meta_s.at[k], recv_sem=meta_r.at[place_of],
            device_id=(j, t), device_id_type=MESH,
        )

    meta_start, meta_arrive, meta_sent = spread(meta_copy)
    meta_start()

    halves = [Half(kind, h, y, x, c, t) for kind in (2, 1) for h in (0, 1)]
    ag_mail = [Mail(ag_s.at[n], ag_r.at[n]) for n in range(4)]
    gathers = [
        plane_gather(hf, f2 if hf.kind == 2 else f1, m) for hf, m in zip(halves, ag_mail)
    ]

    def step(generators):
        for g in generators:
            next(g)

    step(gathers)

    chunks = (pl.ds(0, 256), pl.ds(256, 384))

    def hop_copy(n, m, src, dst, k, j, own):
        cols = chunks[m]
        return pltpu.make_async_remote_copy(
            src_ref=src.at[j, :, cols],
            dst_ref=dst.at[dp if own else j, :, cols],
            send_sem=hop_s.at[n, m, k],
            recv_sem=hop_r.at[n, m, dp if own else j],
            device_id=(j, t),
            device_id_type=MESH,
        )

    hops = [
        [spread(functools.partial(hop_copy, n, m, src, dst)) for m in (0, 1)]
        for n, (src, dst) in enumerate(((st1, rv1), (st2, rv2)))
    ]

    def hop_send(n, m, value):
        src, dst = ((st1, rv1), (st2, rv2))[n]
        src[:, :, chunks[m]] = value.astype(BF).reshape(NDP, TOK, chunks[m].size)
        hops[n][m][0]()
        dst[dp, :, chunks[m]] = src[dp, :, chunks[m]]

    def selector(count, key):
        n = key.shape[1]
        r, q = iota((count, n), 0), iota((count, n), 1)
        hit = ((r >> 4).astype(F32) == key) & ((r & 15) == (q & 15))
        return jnp.where(hit, 1.0, 0.0).astype(BF)

    def widen(column, n):
        k = column.shape[0]
        return jnp.sum(
            jnp.where(iota((k, n), 0) == (iota((k, n), 1) >> 4), column, 0.0), axis=0, keepdims=True
        )

    slots = jnp.sum(
        jnp.where(iota((32, 128), 0) == iota((32, 128), 1), table[0:1].astype(F32), 0.0),
        axis=1,
        keepdims=True,
    )
    to_dest = selector(NDP * TOK, widen(slots, SRC * TOK))
    factor = jnp.sum(
        jnp.where(iota((160, DM), 1) == iota((160, DM), 0) + t * 160, gain[...], 0.0),
        axis=1,
        keepdims=True,
    )
    for k in range(1, NZ):
        sq_copy(k, lax.rem(t + k, NZ), False).wait_recv()
    scale = lax.rsqrt(jnp.sum(sq[...], axis=0) * (1.0 / DM) + 1e-06)
    normed = (patches_t[...].astype(F32) * scale * factor).astype(BF).astype(F32)
    flat[0] = normed[:128].T
    flat[1] = jnp.concatenate([normed[128:], jnp.zeros((96, SRC * WIN), F32)], axis=0).T
    pieces = []
    for p in range(4):
        pieces.append(flat[0, pl.ds(p, SRC * TOK, stride=4), :])
        pieces.append(flat[1, pl.ds(p, SRC * TOK, stride=4), :][:, :32])
    windows = jnp.concatenate(pieces, axis=1).astype(BF)
    hop_send(0, 0, dot(to_dest, windows[:, :256]))
    hop_send(0, 1, dot(to_dest, windows[:, 256:]))
    step(gathers)

    meta_arrive()
    dests, places = meta[:, 0, :], meta[:, 1, :]
    owners = places >> 9
    onward = (
        jnp.sum(jnp.where(dests == dp, (owners + 1).astype(F32), 0.0), axis=1, keepdims=True) - 1.0
    )
    to_owner = selector(NDP * TOK, widen(onward, NDP * TOK))
    via = jnp.where(owners == dp, dests, -1)
    next_place = (places + 1).astype(F32)
    r, q = iota((32, 128), 0), iota((32, 128), 1)
    found = jnp.zeros((32, 128), F32)
    for d in range(NDP):
        found = jnp.where(
            r == d, jnp.sum(jnp.where(via == d, next_place, 0.0), axis=0, keepdims=True), found
        )
    found = jnp.sum(found, axis=1, keepdims=True)
    live = jnp.where(found > 0.5, 1.0, 0.0)
    live_row = jnp.sum(jnp.where(r == q, live, 0.0), axis=0, keepdims=True)
    rank = jnp.sum(jnp.where(q < r, live_row, 0.0), axis=1, keepdims=True)
    rank = jnp.where(found > 0.5, rank, -1.0)
    rank_row = jnp.sum(jnp.where(r == q, rank, 0.0), axis=0, keepdims=True)
    rank_row = jnp.where(iota((1, 128), 1) < NDP, rank_row, -1.0)
    found_row = jnp.sum(jnp.where(r == q, found, 0.0), axis=0, keepdims=True)
    to_work = selector(NTOK, widen(rank, NDP * TOK))

    base = dp * LM + 1
    r, q = iota((32, NTOK), 0), iota((32, NTOK), 1)
    tok_row = jnp.sum(jnp.where(rank == (q >> 4).astype(F32), found, 0.0), axis=0, keepdims=True)
    tok_row = tok_row.astype(jnp.int32) + (iota((1, NTOK), 1) & 15) - base
    r = iota((NTOK, 128), 0)
    tok_col = jnp.sum(
        jnp.where(rank_row == (r >> 4).astype(F32), found_row, 0.0), axis=1, keepdims=True
    )
    tok_col = tok_col.astype(jnp.int32) + (iota((NTOK, 1), 0) & 15) - base
    fetch = jnp.where(iota((NTOK, LM), 1) == tok_col, 1.0, 0.0).astype(BF)
    place[...] = jnp.where(iota((LM, NTOK), 0) == tok_row, 1.0, 0.0).astype(BF)

    for m in (0, 1):
        hops[0][m][1]()
        part = rv1[:, :, chunks[m]].reshape(NDP * TOK, chunks[m].size)
        hop_send(1, m, dot(to_owner, part))
    step(gathers)
    up_rows[...] = dot(fetch, lmg[...]).astype(BF)

    low, high, every = pl.ds(0, 128), pl.ds(128, 128), pl.ds(0, 256)
    zx_mail = [Mail(zx_s.at[m], zx_r.at[m]) for m in (0, 1)]
    zx = []
    for m, cols in enumerate(chunks):
        hops[1][m][1]()
        part = rv2[:, :, cols].reshape(NDP * TOK, cols.size)
        xs[t, :, cols] = dot(to_work, part).astype(BF)
        zx.append(
            ring_gather(dp, t, xs, ((every, cols), (low, cols), (high, cols)), zx_mail[m])
        )
        next(zx[m])
    x_order = [0]
    for _ in range(3):
        step(zx[:1])
        x_order += list(next(zx[1]))
        step(gathers)

    def second_rows(k):
        two = lax.rem(k, 2) * 2
        return f2[lax.div(k, 2), pl.ds(two, 2)].reshape(HID, OUT)

    def back(k, carry):
        hb[k] = dot(second_rows(k), up_rows[...], 1, 1).astype(BF)
        return carry

    lax.fori_loop(0, NZ, back, 0)

    zb_mail = Mail(zb_s, zb_r)

    def put_back(total):
        acc[:HID, :] = total

    zb = ring_scatter(dp, t, hb, hb_room, zb_mail, put_back)
    next(zb)

    def first_part(k):
        j = turn(t, k, NZ)
        w = f1[lax.div(j, 2), lax.rem(j, 2)].reshape(FEAT, HID)
        return dot(xs[j], w)

    z1 = None
    for k in x_order:
        term = first_part(k)
        z1 = term if z1 is None else z1 + term
    step(zx)
    z1 = z1 + first_part(4)
    z1 = jnp.concatenate([z1, jnp.zeros((NTOK, HPAD - HID), F32)], axis=1).T[:HID]
    cdf = 0.5 * (1.0 + lax.erf(z1 * 0.7071067811865476))
    hid[t] = (z1 * cdf).astype(BF)

    zh_mail = Mail(zh_s, zh_r)
    zh = ring_gather(
        dp, t, hid, ((pl.ds(0, 320), every), (pl.ds(0, 160), every), (pl.ds(160, 160), every)), zh_mail
    )
    core_mail = Mail(co_s, co_r)
    sent = []

    def use_hidden(k):
        j = turn(t, k, NZ)
        h = hid[j]
        yy, two = lax.div(j, 2), pl.ds(lax.rem(j, 2) * 2, 2)
        p2[yy, two] = dot(h, up_rows[...]).astype(BF).reshape(2, 2, 80, OUT)
        core_mail.send(p2.at[yy, two, 1 - c], b_cores.at[yy, two], len(sent), sibling)
        sent.append((yy, two))
        term = dot(h, second_rows(j), 0, 0)
        if k == 0:
            mixed[...] = term
        else:
            mixed[...] += term

    summed = []

    def join_cores():
        while len(summed) < len(sent):
            yy, two = sent[len(summed)]
            core_mail.wait(b_cores.at[yy, two], len(summed), sibling)
            mine = p2.at[yy, two, c]
            mine[...] = (mine[...].astype(F32) + b_cores[yy, two].astype(F32)).astype(BF)
            summed.append(yy)

    order = next(zh)
    slope[...] = cdf + z1 * (jnp.exp(-0.5 * z1 * z1) * 0.3989422804014327)
    next(zb)
    for k in order:
        use_hidden(k)
    for order in zh:
        next(zb, None)
        join_cores()
        for k in order:
            use_hidden(k)

    rs_mail = [Mail(rs_s.at[n], rs_r.at[n]) for n in range(4)]

    def put2(h):
        def put(total):
            g2_out[:, 512 * h : 512 * h + 512] = total

        return put

    def put1(h):
        def put(total):
            g1_out[80 * h : 80 * h + 80, :] = total

        return put

    sums = []
    for n, hf in enumerate(halves):
        h = hf.h
        if hf.kind == 2:
            room = (b_sub.at[h, 0], b_sub.at[h, 1], b_full.at[h],
                    b_lasts.at[h, 0], b_lasts.at[h, 1], b_last.at[h])
            sums.append(ring_sums(hf, p2, room, rs_mail[n], put2(h)))
        else:
            room = (a_sub0.at[h], a_sub1.at[h], a_full.at[h],
                    a_last0.at[h], a_last1.at[h], a_last.at[h])
            sums.append(ring_sums(hf, p1, room, rs_mail[n], put1(h)))
    join_cores()
    step(sums[:2])

    for _ in zb:
        pass
    dz_t = acc[:HID, :] * slope[...]
    dz[...] = jnp.concatenate([dz_t, jnp.zeros((HPAD - HID, NTOK), F32)], axis=0).T.astype(BF)

    def grad1(xx, cc):
        term = dot(xs[xx * 2 + cc], dz[:, :HID], 0, 0).astype(BF)
        p1[xx, cc] = term.reshape(4, 160, HID)

    for xx in range(4):
        grad1(xx, 1 - c)
        core_mail.send(p1.at[xx, 1 - c], a_cores.at[xx], 8 + xx, sibling)
    for xx in range(4):
        grad1(xx, c)
        core_mail.wait(a_cores.at[xx], 8 + xx, sibling)
        mine = p1.at[xx, c]
        mine[...] = (mine[...].astype(F32) + a_cores[xx].astype(F32)).astype(BF)
    step(sums[2:])
    step(sums[:2])

    merged = mixed[...].astype(BF)
    covered = jnp.max(place[...].astype(F32), axis=1, keepdims=True) > 0.5
    lm_out[...] = jnp.where(covered, dot(place[...], merged), text[...].astype(F32)).astype(BF)

    for _ in range(3):
        step(sums[2:])
        step(sums[:2])
    step(sums[2:])

    for k in range(1, NZ):
        sq_copy(k, lax.rem(t + k, NZ), True).wait_send()
    meta_sent()
    for n in (0, 1):
        for m in (0, 1):
            hops[n][m][2]()
    for m in ag_mail + rs_mail + zx_mail + [zh_mail, zb_mail, core_mail]:
        m.finish()


def per_device(patches, gain, window_dest, window_pos, fc1, fc2, text_embeds, lm_grad):
    vm = pl.BlockSpec(memory_space=pltpu.VMEM)
    sm = pl.BlockSpec(memory_space=pltpu.SMEM)
    V = pltpu.VMEM
    D = pltpu.SemaphoreType.DMA
    scratch = [
        V((NZ, 1, SRC * WIN), F32),
        V((NDP, 8, 128), jnp.int32),
        V((2, SRC * WIN, 128), F32),
        V((NDP, TOK, FEAT), BF),
        V((NDP, TOK, FEAT), BF),
        V((NDP, TOK, FEAT), BF),
        V((NDP, TOK, FEAT), BF),
        V((NZ, NTOK, FEAT), BF),
        V((4, 2, 4, 160, HID), BF),
        V((4, 4, 2, 80, OUT), BF),
        V((NTOK, OUT), BF),
        V((LM, NTOK), BF),
        V((HID, NTOK), F32),
        V((HID, NTOK), F32),
        V((NZ, HID, NTOK), BF),
        V((NZ, HID, NTOK), BF),
        V((8, HID, NTOK), BF),
        V((NTOK, HPAD), BF),
        V((NTOK, OUT), F32),
        V((4, 2, 4, 160, HID), BF),
        V((4, 4, 2, 80, OUT), BF),
        V((4, 4, 160, HID), BF),
        V((2, 4, 48, HID), BF),
        V((2, 4, 32, HID), BF),
        V((2, 2, 4, 80, HID), BF),
        V((2, 48, HID), BF),
        V((2, 32, HID), BF),
        V((2, 2, 80, HID), BF),
        V((4, 4, 80, OUT), BF),
        V((2, 2, 4, 80, 256), BF),
        V((2, 2, 4, 80, 512), BF),
        V((2, 2, 80, 256), BF),
        V((2, 2, 80, 512), BF),
        D((NZ,)), D((NZ,)),
        D((NDP,)), D((NDP,)),
        D((2, 2, NDP)), D((2, 2, NDP)),
        D((4, 12)), D((4, 12)),
        D((2, 8)), D((2, 8)),
        D((8,)), D((8,)),
        D((8,)), D((8,)),
        D((12,)), D((12,)),
        D((4, 20)), D((4, 20)),
    ]
    return pl.pallas_call(
        body,
        out_shape=(
            jax.ShapeDtypeStruct((LM, OUT), BF),
            jax.ShapeDtypeStruct((160, HID), F32),
            jax.ShapeDtypeStruct((80, OUT), F32),
        ),
        in_specs=[vm, vm, sm, sm, vm, vm, vm, vm],
        out_specs=(vm, vm, vm),
        scratch_shapes=scratch,
        compiler_params=pltpu.CompilerParams(
            collective_id=0, has_side_effects=True, vmem_limit_bytes=60 * 1024 * 1024
        ),
        cost_estimate=pl.CostEstimate(
            flops=6_000_000_000, bytes_accessed=8_000_000, transcendentals=300_000
        ),
    )(patches.T, gain.reshape(1, DM), window_dest, window_pos, fc1, fc2, text_embeds, lm_grad)


def solution(mesh):
    both = P("dp", "tensor")
    return jax.shard_map(
        per_device,
        mesh=mesh,
        in_specs=(both, P(), P("dp"), P("dp"), both, both, both, both),
        out_specs=(both, both, both),
        check_vma=False,
    )
```

time: 152 us -> 137 us (0.901)
  Pallas kernels: 139 us -> 128 us
  other arithmetic: 3.23 us -> 0 us
  local copies, waits for them, and re-layouts: 7.84 us -> 5.39 us
    pallas_call x1, Pallas kernels: 139 us -> 128 us  [per_device(): pl.pallas_call(body, out_shape=(jax.ShapeDtypeStruct((LM, OUT), BF), jax....]
    unnamed x8 -> x7, local copies, waits for them, and re-layouts: 5.05 us -> 4.09 us
where the time goes in v2:
time: 137 us; the launch traced here: 134 us
  Pallas kernels  128 us (93%)
  local copies, waits for them, and re-layouts  5.39 us (4%)
    pallas_call x1, Pallas kernels, per_device(): pl.pallas_call(body, out_shape=(jax.ShapeDtypeStruct((LM, OUT), BF), jax....  128 us
    unnamed x7, local copies, waits for them, and re-layouts  4.09 us

profile of v2, /device:TPU:2, one launch (start us, length us, event | category | flops | bytes accessed | tf_op | source)
XLA Modules:
  0.0 134.3 jit_solution(14912716197670656050)
XLA Ops:
  0.6 1.3 reshape.9.gain
  1.9 128.3 %shard_map.103 = (bf16[512,1024]{1,0:T(8,128)(2,1)}, f32[160,320]{1,0:T(8,128)}, f32[80,1024]{1,0:T(8,128)}) custom-call(bf16[160,1536]{1,0:T(8,128)(2,1)} %bitcast.1, f32[1,1280]{1,0:T(1,128)} %reshape.9.gain, s32[24]{0:T(128)} %dest.1, s32[24]{0:T(128)} %pos.1, bf16[160,320]{1,0:T(8,128)(2,1)} %fc1.1, bf16[80,1024]{1,0:T(8,128)(2,1)} %fc2.1, ...), custom_call_target="tpu_custom_call" | custom-call | flops 6000000000 | bytes 8000000 | tf_op jit(solution)/shard_map/pallas_call | solution.py:680
  130.2 0.0 copy-start.1
  130.2 2.3 %copy.14 = bf16[512,1024]{1,0:T(8,128)(2,1)} copy(bf16[512,1024]{1,0:T(8,128)(2,1)} %get-tuple-element.6) | data formatting | bytes 2097152
  132.5 0.0 copy-done.1
  132.5 0.0 copy-start
  132.5 0.7 copy.15
  133.2 0.4 copy-done
  133.6 0.7 copy.16
Async XLA Ops:
  130.2 2.3 %copy-start.1 = (f32[160,320]{1,0:T(8,128)S(1)}, f32[160,320]{1,0:T(8,128)}, u32[]{:S(2)}) copy-start(f32[160,320]{1,0:T(8,128)} %get-tuple-element.7) | copy-start | bytes 614404
  132.5 1.1 copy-start

commit v3 on v2

--- a/solution.py
+++ b/solution.py
@@ -93,26 +93,27 @@
 
 
 class Mail:
-    def __init__(self, send, recv):
-        self.s, self.r, self.started = send, recv, []
-
-    def make(self, src, dst, i, device):
+    def __init__(self, pool, first, recv):
+        self.pool, self.next, self.r, self.started = pool, first, recv, []
+
+    def make(self, src, dst, send, i, device):
         return pltpu.make_async_remote_copy(
             src_ref=src,
             dst_ref=dst,
-            send_sem=self.s.at[i],
+            send_sem=self.pool.at[send],
             recv_sem=self.r.at[i],
             device_id=device,
             device_id_type=MESH,
         )
 
     def send(self, src, dst, i, device):
-        copy = self.make(src, dst, i, device)
+        copy = self.make(src, dst, self.next, i, device)
         copy.start()
+        self.next += 1
         self.started.append(copy)
 
     def wait(self, dst, i, device):
-        self.make(dst, dst, i, device).wait_recv()
+        self.make(dst, dst, 0, i, device).wait_recv()
 
     def finish(self):
         for copy in self.started:
@@ -143,17 +144,16 @@
     yield
     wait(hf.group(buf, -1), 4)
     send(hf.group(buf, -1, 0), 7, hf.second(1))
-    send(hf.group(buf, -1), 8, hf.sibling())
+    send(hf.group(buf, -1), 6, hf.sibling())
     wait(hf.group(buf, 1), 5)
-    send(hf.group(buf, 1, 1), 9, hf.second(-1))
-    send(hf.group(buf, 1), 10, hf.sibling())
+    send(hf.group(buf, 1, 1), 8, hf.second(-1))
+    send(hf.group(buf, 1), 6, hf.sibling())
     yield
     wait(hf.group(buf, 2, 0), 7)
-    wait(hf.group(buf, 2, 1), 9)
-    send(hf.group(buf, 2), 11, hf.sibling())
-    yield
-    for k, i in ((0, 6), (-1, 8), (1, 10), (2, 11)):
-        wait(hf.group(buf, k, None, True), i)
+    wait(hf.group(buf, 2, 1), 8)
+    send(hf.group(buf, 2), 6, hf.sibling())
+    yield
+    wait(hf.at(buf, slice(None), slice(None), 1 - hf.c, None), 6)
     yield
 
 
@@ -240,52 +240,59 @@
     yield (4,)
 
 
-def ring_scatter(dp, t, buf, room, mail, put):
+def ring_scatter(dp, t, buf, room, cols, mail, put):
     up, down = (dp, turn(t, 1, NZ)), (dp, turn(t, -1, NZ))
     half = HID // 2
-    low, high = pl.ds(0, half), pl.ds(half, half)
+    low, high, every = pl.ds(0, half), pl.ds(half, half), pl.ds(0, HID)
 
     def view(k, cut):
-        return buf.at[turn(t, k, NZ), cut, :]
+        return buf.at[turn(t, k, NZ), cut, cols]
 
     def plus(k, cut, other):
         mine = view(k, cut)
         mine[...] = (mine[...].astype(F32) + other[...].astype(F32)).astype(BF)
 
-    mail.send(view(4, low), room.at[0, low, :], 0, up)
-    mail.send(view(4, high), room.at[1, high, :], 1, down)
-    yield
-    every = pl.ds(0, HID)
+    mail.send(view(4, low), room.at[0, low, cols], 0, up)
+    mail.send(view(4, high), room.at[1, high, cols], 1, down)
+    yield
     for n, k in enumerate((3, 2, 1)):
         a, b = (low, high) if n == 0 else (every, every)
-        mail.wait(room.at[2 * n, a, :], 2 * n, up)
-        plus(k, a, room.at[2 * n, a, :])
-        mail.send(view(k, every), room.at[2 * n + 2], 2 * n + 2, up)
-        mail.wait(room.at[2 * n + 1, b, :], 2 * n + 1, up)
-        plus(-k, b, room.at[2 * n + 1, b, :])
-        mail.send(view(-k, every), room.at[2 * n + 3], 2 * n + 3, down)
+        mail.wait(room.at[2 * n, a, cols], 2 * n, up)
+        plus(k, a, room.at[2 * n, a, cols])
+        mail.send(view(k, every), room.at[2 * n + 2, every, cols], 2 * n + 2, up)
+        mail.wait(room.at[2 * n + 1, b, cols], 2 * n + 1, up)
+        plus(-k, b, room.at[2 * n + 1, b, cols])
+        mail.send(view(-k, every), room.at[2 * n + 3, every, cols], 2 * n + 3, down)
         yield
-    mail.wait(room.at[6], 6, up)
-    mail.wait(room.at[7], 7, up)
-    put(view(0, every)[...].astype(F32) + room[6].astype(F32) + room[7].astype(F32))
+    mail.wait(room.at[6, every, cols], 6, up)
+    mail.wait(room.at[7, every, cols], 7, up)
+    put(
+        view(0, every)[...].astype(F32)
+        + room[6, :, cols].astype(F32)
+        + room[7, :, cols].astype(F32)
+    )
     yield
 
 
 def body(
-    patches_t, gain, dest, pos, fc1, fc2, text, lmg,
-    lm_out, g1_out, g2_out,
-    sq, meta, flat, st1, rv1, st2, rv2, xs, f1, f2, up_rows, place,
-    acc, slope, hid, hb, hb_room, dz, mixed, p1, p2,
+    patches_t, gain, dest, pos, fc1, fc2, text_hbm, lmg_hbm,
+    lm_hbm, g1_out, g2_out,
+    text, lmg, lm_out, io_s,
+    sq, meta, gains, factor, xn, flat, st1, rv1, st2, rv2, xs, f1, f2, up_rows, place,
+    acc, hid, hb, hb_room, dz, mixed, p1, p2,
     a_cores, a_sub0, a_sub1, a_full, a_last0, a_last1, a_last,
     b_cores, b_sub, b_full, b_lasts, b_last,
-    sq_s, sq_r, meta_s, meta_r, hop_s, hop_r, ag_s, ag_r, zx_s, zx_r, zh_s, zh_r, zb_s, zb_r,
-    co_s, co_r, rs_s, rs_r,
+    pool, sq_s, meta_s, hop_s, ag_r, zx_r, zh_r, zb_r, co_r, rs_r,
 ):
     dp = lax.axis_index("dp")
     t = lax.axis_index("tensor")
     y, x, c = lax.div(dp, 8), lax.rem(lax.div(dp, 2), 4), lax.rem(dp, 2)
     sibling = (y * 8 + x * 2 + 1 - c, t)
 
+    text_in = pltpu.make_async_copy(text_hbm, text, io_s.at[0])
+    lmg_in = pltpu.make_async_copy(lmg_hbm, lmg, io_s.at[1])
+    lm_done = pltpu.make_async_copy(lm_out, lm_hbm, io_s.at[2])
+
     barrier = pltpu.get_barrier_semaphore()
 
     def greet(k, carry):
@@ -304,89 +311,16 @@
 
     lax.fori_loop(1, NZ, greet_z, 0)
 
-    r, q = iota((8, 128), 0), iota((8, 128), 1)
-    table = jnp.full((8, 128), -1, jnp.int32)
+    lmg_in.start()
+    text_in.start()
+
+    q = iota((1, 128), 1)
+    table = jnp.full((1, 128), -1, jnp.int32)
     for s in range(SRC):
-        table = jnp.where(q == s, jnp.where(r == 0, dest[s], pos[s]), table)
+        table = jnp.where(q == s, jnp.where(dest[s] >= 0, (dest[s] << 14) + pos[s], -1), table)
     meta[dp] = table
-
-    value = patches_t[...].astype(F32)
-    sq[t] = jnp.sum(value * value, axis=0, keepdims=True)
     f2[y, x, c] = fc2[...]
     f1[x, c, y] = fc1[...]
-
-    pl.semaphore_wait(barrier, NDP - 1 + NZ - 1)
-
-    def sq_copy(k, j, own):
-        place_of = t if own else j
-        return pltpu.make_async_remote_copy(
-            src_ref=sq.at[place_of], dst_ref=sq.at[place_of], send_sem=sq_s.at[k], recv_sem=sq_r.at[place_of],
-            device_id=(dp, j), device_id_type=MESH,
-        )
-
-    for k in range(1, NZ):
-        sq_copy(k, lax.rem(t + k, NZ), True).start()
-
-    def spread(copy):
-        def start(k, carry):
-            copy(k, lax.rem(dp + k, NDP), True).start()
-            return carry
-
-        def arrive(k, carry):
-            copy(k, lax.rem(dp + k, NDP), False).wait_recv()
-            return carry
-
-        def sent(k, carry):
-            copy(k, lax.rem(dp + k, NDP), True).wait_send()
-            return carry
-
-        return [functools.partial(lax.fori_loop, 1, NDP, f, 0) for f in (start, arrive, sent)]
-
-    def meta_copy(k, j, own):
-        place_of = dp if own else j
-        return pltpu.make_async_remote_copy(
-            src_ref=meta.at[place_of], dst_ref=meta.at[place_of], send_sem=meta_s.at[k], recv_sem=meta_r.at[place_of],
-            device_id=(j, t), device_id_type=MESH,
-        )
-
-    meta_start, meta_arrive, meta_sent = spread(meta_copy)
-    meta_start()
-
-    halves = [Half(kind, h, y, x, c, t) for kind in (2, 1) for h in (0, 1)]
-    ag_mail = [Mail(ag_s.at[n], ag_r.at[n]) for n in range(4)]
-    gathers = [
-        plane_gather(hf, f2 if hf.kind == 2 else f1, m) for hf, m in zip(halves, ag_mail)
-    ]
-
-    def step(generators):
-        for g in generators:
-            next(g)
-
-    step(gathers)
-
-    chunks = (pl.ds(0, 256), pl.ds(256, 384))
-
-    def hop_copy(n, m, src, dst, k, j, own):
-        cols = chunks[m]
-        return pltpu.make_async_remote_copy(
-            src_ref=src.at[j, :, cols],
-            dst_ref=dst.at[dp if own else j, :, cols],
-            send_sem=hop_s.at[n, m, k],
-            recv_sem=hop_r.at[n, m, dp if own else j],
-            device_id=(j, t),
-            device_id_type=MESH,
-        )
-
-    hops = [
-        [spread(functools.partial(hop_copy, n, m, src, dst)) for m in (0, 1)]
-        for n, (src, dst) in enumerate(((st1, rv1), (st2, rv2)))
-    ]
-
-    def hop_send(n, m, value):
-        src, dst = ((st1, rv1), (st2, rv2))[n]
-        src[:, :, chunks[m]] = value.astype(BF).reshape(NDP, TOK, chunks[m].size)
-        hops[n][m][0]()
-        dst[dp, :, chunks[m]] = src[dp, :, chunks[m]]
 
     def selector(count, key):
         n = key.shape[1]
@@ -400,35 +334,82 @@
             jnp.where(iota((k, n), 0) == (iota((k, n), 1) >> 4), column, 0.0), axis=0, keepdims=True
         )
 
-    slots = jnp.sum(
-        jnp.where(iota((32, 128), 0) == iota((32, 128), 1), table[0:1].astype(F32), 0.0),
-        axis=1,
-        keepdims=True,
-    )
-    to_dest = selector(NDP * TOK, widen(slots, SRC * TOK))
-    factor = jnp.sum(
-        jnp.where(iota((160, DM), 1) == iota((160, DM), 0) + t * 160, gain[...], 0.0),
-        axis=1,
-        keepdims=True,
-    )
-    for k in range(1, NZ):
-        sq_copy(k, lax.rem(t + k, NZ), False).wait_recv()
-    scale = lax.rsqrt(jnp.sum(sq[...], axis=0) * (1.0 / DM) + 1e-06)
-    normed = (patches_t[...].astype(F32) * scale * factor).astype(BF).astype(F32)
-    flat[0] = normed[:128].T
-    flat[1] = jnp.concatenate([normed[128:], jnp.zeros((96, SRC * WIN), F32)], axis=0).T
+    value = patches_t[...].astype(F32)
+    flat[0] = value[:128].T
+    flat[1] = jnp.concatenate([value[128:], jnp.zeros((96, SRC * WIN), F32)], axis=0).T
     pieces = []
     for p in range(4):
         pieces.append(flat[0, pl.ds(p, SRC * TOK, stride=4), :])
         pieces.append(flat[1, pl.ds(p, SRC * TOK, stride=4), :][:, :32])
     windows = jnp.concatenate(pieces, axis=1).astype(BF)
-    hop_send(0, 0, dot(to_dest, windows[:, :256]))
-    hop_send(0, 1, dot(to_dest, windows[:, 256:]))
+    slots = jnp.sum(
+        jnp.where(iota((32, 128), 0) == iota((32, 128), 1), (table >> 14).astype(F32), 0.0),
+        axis=1,
+        keepdims=True,
+    )
+    to_dest = selector(NDP * TOK, widen(slots, SRC * TOK))
+    st1[...] = dot(to_dest, windows).astype(BF).reshape(NDP, TOK, FEAT)
+    rv1[dp] = st1[dp]
+
+    pl.semaphore_wait(barrier, NDP - 1 + NZ - 1)
+
+    def spread(copy, many):
+        def start(k, carry):
+            copy(k, lax.rem(dp + k, NDP)).start()
+            return carry
+
+        return (
+            functools.partial(lax.fori_loop, 1, NDP, start, 0),
+            lambda: many().wait_recv(),
+            lambda: many().wait_send(),
+        )
+
+    def push(src, dst, sems, device):
+        return pltpu.make_async_remote_copy(
+            src_ref=src, dst_ref=dst, send_sem=sems.at[0], recv_sem=sems.at[1],
+            device_id=device, device_id_type=MESH,
+        )
+
+    others = pl.ds(0, NDP - 1)
+    meta_start, meta_arrive, meta_sent = spread(
+        lambda k, j: push(meta.at[dp], meta.at[dp], meta_s, (j, t)),
+        lambda: push(meta.at[others], meta.at[others], meta_s, sibling),
+    )
+
+    chunks = (pl.ds(0, 256), pl.ds(256, 384))
+
+    def hop(n, m, src, dst):
+        cols, sems = chunks[m], hop_s.at[2 * n + m]
+        return spread(
+            lambda k, j: push(src.at[j, :, cols], dst.at[dp, :, cols], sems, (j, t)),
+            lambda: push(src.at[others, :, cols], dst.at[others, :, cols], sems, sibling),
+        )
+
+    hops = [
+        [hop(n, m, src, dst) for m in (0, 1)]
+        for n, (src, dst) in enumerate(((st1, rv1), (st2, rv2)))
+    ]
+
+    meta_start()
+    hops[0][0][0]()
+    hops[0][1][0]()
+
+    halves = [Half(kind, h, y, x, c, t) for kind in (2, 1) for h in (0, 1)]
+    ag_mail = [Mail(pool, 12 * n, ag_r.at[n]) for n in range(4)]
+    gathers = [
+        plane_gather(hf, f2 if hf.kind == 2 else f1, m) for hf, m in zip(halves, ag_mail)
+    ]
+
+    def step(generators):
+        for g in generators:
+            next(g)
+
     step(gathers)
 
     meta_arrive()
-    dests, places = meta[:, 0, :], meta[:, 1, :]
-    owners = places >> 9
+    tables = meta[:, 0, :]
+    dests, places = tables >> 14, tables & 16383
+    owners = jnp.where(tables >= 0, places >> 9, -1)
     onward = (
         jnp.sum(jnp.where(dests == dp, (owners + 1).astype(F32), 0.0), axis=1, keepdims=True) - 1.0
     )
@@ -463,15 +444,18 @@
     fetch = jnp.where(iota((NTOK, LM), 1) == tok_col, 1.0, 0.0).astype(BF)
     place[...] = jnp.where(iota((LM, NTOK), 0) == tok_row, 1.0, 0.0).astype(BF)
 
-    for m in (0, 1):
+
+    for m, cols in enumerate(chunks):
         hops[0][m][1]()
-        part = rv1[:, :, chunks[m]].reshape(NDP * TOK, chunks[m].size)
-        hop_send(1, m, dot(to_owner, part))
-    step(gathers)
+        part = rv1[:, :, cols].reshape(NDP * TOK, cols.size)
+        st2[:, :, cols] = dot(to_owner, part).astype(BF).reshape(NDP, TOK, cols.size)
+        hops[1][m][0]()
+        rv2[dp, :, cols] = st2[dp, :, cols]
+    lmg_in.wait()
     up_rows[...] = dot(fetch, lmg[...]).astype(BF)
 
     low, high, every = pl.ds(0, 128), pl.ds(128, 128), pl.ds(0, 256)
-    zx_mail = [Mail(zx_s.at[m], zx_r.at[m]) for m in (0, 1)]
+    zx_mail = [Mail(pool, 48 + 8 * m, zx_r.at[m]) for m in (0, 1)]
     zx = []
     for m, cols in enumerate(chunks):
         hops[1][m][1]()
@@ -481,11 +465,48 @@
             ring_gather(dp, t, xs, ((every, cols), (low, cols), (high, cols)), zx_mail[m])
         )
         next(zx[m])
-    x_order = [0]
-    for _ in range(3):
-        step(zx[:1])
-        x_order += list(next(zx[1]))
-        step(gathers)
+
+    seg = iota((NTOK, FEAT), 1) // 160
+    square = xs[t].astype(F32)
+    square = square * square
+    lane = iota((NTOK, 128), 1)
+    sums_of = jnp.zeros((NTOK, 128), F32)
+    for p in range(4):
+        part = jnp.sum(jnp.where(seg == p, square, 0.0), axis=1, keepdims=True)
+        sums_of = jnp.where(lane == p, part, sums_of)
+    sq[t] = sums_of.T[:8]
+
+    for k in range(1, NZ):
+        push(sq.at[t], sq.at[t], sq_s, (dp, lax.rem(t + k, NZ))).start()
+    seven = push(sq.at[pl.ds(0, NZ - 1)], sq.at[pl.ds(0, NZ - 1)], sq_s, sibling)
+    step(gathers)
+    step(gathers)
+    all_gain = gain[...].reshape(1, DM)
+    for k in range(NZ):
+        gains[k] = jnp.concatenate([all_gain[:, 160 * k : 160 * k + 160]] * 4, axis=1)
+    seven.wait_recv()
+    scale = lax.rsqrt(jnp.sum(sq[...], axis=0) * (1.0 / DM) + 1e-06)
+    scale = jnp.concatenate([scale] * 16, axis=0).T
+    factor[...] = jnp.where(
+        seg == 0,
+        scale[:, 0:1],
+        jnp.where(seg == 1, scale[:, 1:2], jnp.where(seg == 2, scale[:, 2:3], scale[:, 3:4])),
+    )
+
+    def normalise(k):
+        j = turn(t, k, NZ)
+        xn[j] = (xs[j].astype(F32) * factor[...] * gains[j]).astype(BF)
+
+    normalise(0)
+    step(zx)
+    step(gathers)
+    normalise(-1)
+    normalise(1)
+    step(zx)
+    step(gathers)
+    normalise(-2)
+    normalise(2)
+    step(gathers)
 
     def second_rows(k):
         two = lax.rem(k, 2) * 2
@@ -497,48 +518,64 @@
 
     lax.fori_loop(0, NZ, back, 0)
 
-    zb_mail = Mail(zb_s, zb_r)
-
-    def put_back(total):
-        acc[:HID, :] = total
-
-    zb = ring_scatter(dp, t, hb, hb_room, zb_mail, put_back)
-    next(zb)
+    tokens = (low, high)
+    zb_mail = [Mail(pool, 64 + 8 * m, zb_r.at[m]) for m in (0, 1)]
+
+    def put_back(m):
+        def put(total):
+            acc[:, 128 * m : 128 * m + 128] = total
+
+        return put
+
+    zb = [
+        ring_scatter(dp, t, hb, hb_room, tokens[m], zb_mail[m], put_back(m)) for m in (0, 1)
+    ]
+    step(zb)
 
     def first_part(k):
         j = turn(t, k, NZ)
         w = f1[lax.div(j, 2), lax.rem(j, 2)].reshape(FEAT, HID)
-        return dot(xs[j], w)
-
-    z1 = None
-    for k in x_order:
-        term = first_part(k)
-        z1 = term if z1 is None else z1 + term
+        return dot(xn[j], w)
+
     step(zx)
+    normalise(-3)
+    normalise(3)
+    meta_sent()
+    seven.wait_send()
+    for n in (0, 1):
+        for m in (0, 1):
+            hops[n][m][2]()
+    step(zb)
+    z1 = first_part(0) + first_part(-1) + first_part(1) + first_part(-2)
+    step(zb)
+    for m in ag_mail:
+        m.finish()
+    z1 = z1 + first_part(2) + first_part(-3) + first_part(3)
+    step(zx)
+    normalise(4)
     z1 = z1 + first_part(4)
     z1 = jnp.concatenate([z1, jnp.zeros((NTOK, HPAD - HID), F32)], axis=1).T[:HID]
     cdf = 0.5 * (1.0 + lax.erf(z1 * 0.7071067811865476))
     hid[t] = (z1 * cdf).astype(BF)
 
-    zh_mail = Mail(zh_s, zh_r)
-    zh = ring_gather(
-        dp, t, hid, ((pl.ds(0, 320), every), (pl.ds(0, 160), every), (pl.ds(160, 160), every)), zh_mail
-    )
-    core_mail = Mail(co_s, co_r)
+    zh_mail = [Mail(pool, 8 * m, zh_r.at[m]) for m in (0, 1)]
+    zh = [
+        ring_gather(
+            dp, t, hid,
+            ((pl.ds(0, 320), cut), (pl.ds(0, 160), cut), (pl.ds(160, 160), cut)),
+            zh_mail[m],
+        )
+        for m, cut in enumerate(tokens)
+    ]
+    core_mail = Mail(pool, 96, co_r)
     sent = []
 
     def use_hidden(k):
         j = turn(t, k, NZ)
-        h = hid[j]
         yy, two = lax.div(j, 2), pl.ds(lax.rem(j, 2) * 2, 2)
-        p2[yy, two] = dot(h, up_rows[...]).astype(BF).reshape(2, 2, 80, OUT)
+        p2[yy, two] = dot(hid[j], up_rows[...]).astype(BF).reshape(2, 2, 80, OUT)
         core_mail.send(p2.at[yy, two, 1 - c], b_cores.at[yy, two], len(sent), sibling)
         sent.append((yy, two))
-        term = dot(h, second_rows(j), 0, 0)
-        if k == 0:
-            mixed[...] = term
-        else:
-            mixed[...] += term
 
     summed = []
 
@@ -550,18 +587,23 @@
             mine[...] = (mine[...].astype(F32) + b_cores[yy, two].astype(F32)).astype(BF)
             summed.append(yy)
 
-    order = next(zh)
-    slope[...] = cdf + z1 * (jnp.exp(-0.5 * z1 * z1) * 0.3989422804014327)
-    next(zb)
-    for k in order:
-        use_hidden(k)
-    for order in zh:
-        next(zb, None)
-        join_cores()
-        for k in order:
-            use_hidden(k)
-
-    rs_mail = [Mail(rs_s.at[n], rs_r.at[n]) for n in range(4)]
+    def grad1(xx, cc):
+        term = dot(xn[xx * 2 + cc], dz[:, :HID], 0, 0).astype(BF)
+        p1[xx, cc] = term.reshape(4, 160, HID)
+
+    step(zh)
+    step(zb)
+    slope = cdf + z1 * (jnp.exp(-0.5 * z1 * z1) * 0.3989422804014327)
+    step(zb)
+    dz_t = acc[...] * slope
+    dz[...] = jnp.concatenate([dz_t, jnp.zeros((HPAD - HID, NTOK), F32)], axis=0).T.astype(BF)
+    for xx in range(4):
+        grad1(xx, 1 - c)
+        core_mail.send(p1.at[xx, 1 - c], a_cores.at[xx], 8 + xx, sibling)
+    use_hidden(0)
+    for m in zx_mail:
+        m.finish()
+    rs_mail = [Mail(pool, (56, 76, 16, 36)[n], rs_r.at[n]) for n in range(4)]
 
     def put2(h):
         def put(total):
@@ -586,56 +628,71 @@
             room = (a_sub0.at[h], a_sub1.at[h], a_full.at[h],
                     a_last0.at[h], a_last1.at[h], a_last.at[h])
             sums.append(ring_sums(hf, p1, room, rs_mail[n], put1(h)))
-    join_cores()
-    step(sums[:2])
-
-    for _ in zb:
-        pass
-    dz_t = acc[:HID, :] * slope[...]
-    dz[...] = jnp.concatenate([dz_t, jnp.zeros((HPAD - HID, NTOK), F32)], axis=0).T.astype(BF)
-
-    def grad1(xx, cc):
-        term = dot(xs[xx * 2 + cc], dz[:, :HID], 0, 0).astype(BF)
-        p1[xx, cc] = term.reshape(4, 160, HID)
-
-    for xx in range(4):
-        grad1(xx, 1 - c)
-        core_mail.send(p1.at[xx, 1 - c], a_cores.at[xx], 8 + xx, sibling)
+    step(zh)
     for xx in range(4):
         grad1(xx, c)
         core_mail.wait(a_cores.at[xx], 8 + xx, sibling)
         mine = p1.at[xx, c]
         mine[...] = (mine[...].astype(F32) + a_cores[xx].astype(F32)).astype(BF)
     step(sums[2:])
+    use_hidden(-1)
+    use_hidden(1)
+    step(zh)
+    use_hidden(-2)
+    use_hidden(2)
+    join_cores()
+    step(sums[2:])
+    step(zh)
+    use_hidden(-3)
+    use_hidden(3)
+    join_cores()
+    for m in zb_mail:
+        m.finish()
+    step(sums[2:])
+    step(zh)
+    use_hidden(4)
+    join_cores()
     step(sums[:2])
-
-    merged = mixed[...].astype(BF)
+    step(sums[2:])
+
+    def forward(k):
+        return dot(hid[k], second_rows(k), 0, 0)
+
+    mixed[...] = forward(0) + forward(1) + forward(2) + forward(3)
+    step(sums[:2])
+    step(sums[2:])
+    merged = (mixed[...] + forward(4) + forward(5) + forward(6) + forward(7)).astype(BF)
+    step(sums[:2])
+    text_in.wait()
     covered = jnp.max(place[...].astype(F32), axis=1, keepdims=True) > 0.5
     lm_out[...] = jnp.where(covered, dot(place[...], merged), text[...].astype(F32)).astype(BF)
-
-    for _ in range(3):
-        step(sums[2:])
-        step(sums[:2])
-    step(sums[2:])
-
-    for k in range(1, NZ):
-        sq_copy(k, lax.rem(t + k, NZ), True).wait_send()
-    meta_sent()
-    for n in (0, 1):
-        for m in (0, 1):
-            hops[n][m][2]()
-    for m in ag_mail + rs_mail + zx_mail + [zh_mail, zb_mail, core_mail]:
+    lm_done.start()
+    step(sums[:2])
+    for m in zh_mail + [core_mail]:
+        m.finish()
+    step(sums[:2])
+
+    lm_done.wait()
+    for m in rs_mail:
         m.finish()
 
 
 def per_device(patches, gain, window_dest, window_pos, fc1, fc2, text_embeds, lm_grad):
     vm = pl.BlockSpec(memory_space=pltpu.VMEM)
+    anywhere = pl.BlockSpec(memory_space=pl.ANY)
     sm = pl.BlockSpec(memory_space=pltpu.SMEM)
     V = pltpu.VMEM
     D = pltpu.SemaphoreType.DMA
     scratch = [
-        V((NZ, 1, SRC * WIN), F32),
-        V((NDP, 8, 128), jnp.int32),
+        V((LM, OUT), BF),
+        V((LM, OUT), BF),
+        V((LM, OUT), BF),
+        D((3,)),
+        V((NZ, 8, NTOK), F32),
+        V((NDP, 1, 128), jnp.int32),
+        V((NZ, 1, FEAT), F32),
+        V((NTOK, FEAT), F32),
+        V((NZ, NTOK, FEAT), BF),
         V((2, SRC * WIN, 128), F32),
         V((NDP, TOK, FEAT), BF),
         V((NDP, TOK, FEAT), BF),
@@ -646,7 +703,6 @@
         V((4, 4, 2, 80, OUT), BF),
         V((NTOK, OUT), BF),
         V((LM, NTOK), BF),
-        V((HID, NTOK), F32),
         V((HID, NTOK), F32),
         V((NZ, HID, NTOK), BF),
         V((NZ, HID, NTOK), BF),
@@ -667,25 +723,18 @@
         V((2, 2, 4, 80, 512), BF),
         V((2, 2, 80, 256), BF),
         V((2, 2, 80, 512), BF),
-        D((NZ,)), D((NZ,)),
-        D((NDP,)), D((NDP,)),
-        D((2, 2, NDP)), D((2, 2, NDP)),
-        D((4, 12)), D((4, 12)),
-        D((2, 8)), D((2, 8)),
-        D((8,)), D((8,)),
-        D((8,)), D((8,)),
-        D((12,)), D((12,)),
-        D((4, 20)), D((4, 20)),
+        D((108,)), D((2,)), D((2,)), D((4, 2)),
+        D((4, 9)), D((2, 8)), D((2, 8)), D((2, 8)), D((12,)), D((4, 20)),
     ]
     return pl.pallas_call(
         body,
         out_shape=(
-            jax.ShapeDtypeStruct((LM, OUT), BF),
-            jax.ShapeDtypeStruct((160, HID), F32),
-            jax.ShapeDtypeStruct((80, OUT), F32),
+            pltpu.VMEM((LM, OUT), BF),
+            pltpu.VMEM((160, HID), F32),
+            pltpu.VMEM((80, OUT), F32),
         ),
-        in_specs=[vm, vm, sm, sm, vm, vm, vm, vm],
-        out_specs=(vm, vm, vm),
+        in_specs=[vm, vm, sm, sm, vm, vm, anywhere, anywhere],
+        out_specs=(anywhere, vm, vm),
         scratch_shapes=scratch,
         compiler_params=pltpu.CompilerParams(
             collective_id=0, has_side_effects=True, vmem_limit_bytes=60 * 1024 * 1024
@@ -693,7 +742,7 @@
         cost_estimate=pl.CostEstimate(
             flops=6_000_000_000, bytes_accessed=8_000_000, transcendentals=300_000
         ),
-    )(patches.T, gain.reshape(1, DM), window_dest, window_pos, fc1, fc2, text_embeds, lm_grad)
+    )(patches.T, gain, window_dest, window_pos, fc1, fc2, text_embeds, lm_grad)
 
 
 def solution(mesh):

time: 137 us -> 128 us (0.934); the launches traced: 134 us -> 127 us
  Pallas kernels: 128 us -> 124 us
  local copies, waits for them, and re-layouts: 5.39 us -> 2.39 us
    pallas_call x1, Pallas kernels: 128 us -> 124 us  [per_device(): pl.pallas_call(body, out_shape=(pltpu.VMEM((LM, OUT), BF), pltpu.VMEM((16...]
    unnamed x7 -> x3, local copies, waits for them, and re-layouts: 4.09 us -> 2.39 us
where the time goes in v3:
time: 128 us; the launch traced here: 127 us
  Pallas kernels  124 us (97%)
  local copies, waits for them, and re-layouts  2.39 us (2%)
    pallas_call x1, Pallas kernels, per_device(): pl.pallas_call(body, out_shape=(pltpu.VMEM((LM, OUT), BF), pltpu.VMEM((16...  124 us

profile of v3, /device:TPU:2, one launch (start us, length us, event | category | flops | bytes accessed | tf_op | source)
XLA Modules:
  0.0 127.3 jit_solution(11914564220616390554)
XLA Ops:
  0.6 124.3 %shard_map.103 = (bf16[512,1024]{1,0:T(8,128)(2,1)S(1)}, f32[160,320]{1,0:T(8,128)S(1)}, f32[80,1024]{1,0:T(8,128)S(1)}) custom-call(bf16[160,1536]{1,0:T(8,128)(2,1)} %bitcast.1, f32[1280]{0:T(1024)} %gain.1, s32[24]{0:T(128)} %dest.1, s32[24]{0:T(128)} %pos.1, bf16[160,320]{1,0:T(8,128)(2,1)} %fc1.1, bf16[80,1024]{1,0:T(8,128)(2,1)} %fc2.1, ...), custom_call_target="tpu_custom_call" | custom-call | flops 6000000000 | bytes 8000000 | tf_op jit(solution)/shard_map/pallas_call | solution.py:729
  124.9 1.0 copy.14
  125.9 0.7 copy.15
  126.6 0.7 copy.16

commit v4 on v3

--- a/solution.py
+++ b/solution.py
@@ -79,10 +79,13 @@
         return self.at(buf, p, self.x, self.c, s)
 
     def cell(self, buf, g, b, s=None):
-        p, q = turn(self.r, g, 4), turn(self.q, b, 4)
-        if self.h == 0:
-            return self.at(buf, p, q, self.c, s)
-        return self.at(buf, q, p, self.c, s)
+        y, x = turn(self.r, g, 4), turn(self.q, b, 4)
+        if self.h == 1:
+            y, x = x, y
+        rows, cols = self.cut(s)
+        if self.kind == 2:
+            return buf.at[y, x, rows, cols]
+        return buf.at[x, y, rows, cols]
 
     def group(self, buf, k, s=None, other=False):
         p = turn(self.r, k, 4)
@@ -187,21 +190,21 @@
         wait(full.at[1, n], 12 + n)
         plus(hf.cell(buf, 0, order[n]), full.at[0, n], full.at[1, n])
         if n == 0:
-            mail.send(hf.block(buf, 2, 0), last0, 16, hf.first(1))
-            mail.send(hf.block(buf, 2, 1), last1, 17, hf.first(-1))
+            mail.send(hf.cell(buf, 0, 2, 0), last0, 16, hf.first(1))
+            mail.send(hf.cell(buf, 0, 2, 1), last1, 17, hf.first(-1))
     yield
     wait(last0, 16)
-    plus(hf.block(buf, 1, 0), last0)
-    mail.send(hf.block(buf, 1), last.at[0], 18, hf.first(1))
+    plus(hf.cell(buf, 0, 1, 0), last0)
+    mail.send(hf.cell(buf, 0, 1), last.at[0], 18, hf.first(1))
     wait(last1, 17)
-    plus(hf.block(buf, -1, 1), last1)
-    mail.send(hf.block(buf, -1), last.at[1], 19, hf.first(-1))
+    plus(hf.cell(buf, 0, -1, 1), last1)
+    mail.send(hf.cell(buf, 0, -1), last.at[1], 19, hf.first(-1))
     yield
     wait(full.at[0, 3], 11)
     wait(full.at[1, 3], 15)
     wait(last.at[0], 18)
     wait(last.at[1], 19)
-    total = hf.block(buf, 0)[...].astype(F32)
+    total = hf.cell(buf, 0, 0)[...].astype(F32)
     for part in (full[0, 3], full[1, 3], last[0], last[1]):
         total = total + part.astype(F32)
     put(total)
@@ -279,9 +282,9 @@
     lm_hbm, g1_out, g2_out,
     text, lmg, lm_out, io_s,
     sq, meta, gains, factor, xn, flat, st1, rv1, st2, rv2, xs, f1, f2, up_rows, place,
-    acc, hid, hb, hb_room, dz, mixed, p1, p2,
-    a_cores, a_sub0, a_sub1, a_full, a_last0, a_last1, a_last,
-    b_cores, b_sub, b_full, b_lasts, b_last,
+    acc, hid, hb, hb_room, dz, mixed, p1, p2, hid2, up2, dz2, x2,
+    a_sub0, a_sub1, a_full, a_last0, a_last1, a_last,
+    b_sub, b_full, b_lasts, b_last,
     pool, sq_s, meta_s, hop_s, ag_r, zx_r, zh_r, zb_r, co_r, rs_r,
 ):
     dp = lax.axis_index("dp")
@@ -451,20 +454,32 @@
         st2[:, :, cols] = dot(to_owner, part).astype(BF).reshape(NDP, TOK, cols.size)
         hops[1][m][0]()
         rv2[dp, :, cols] = st2[dp, :, cols]
+    step(gathers)
     lmg_in.wait()
     up_rows[...] = dot(fetch, lmg[...]).astype(BF)
+    core_mail = Mail(pool, 96, co_r)
+    core_mail.send(up_rows, up2, 8, sibling)
+    all_gain = gain[...].reshape(1, DM)
+    for k in range(NZ):
+        gains[k] = jnp.concatenate([all_gain[:, 160 * k : 160 * k + 160]] * 4, axis=1)
 
     low, high, every = pl.ds(0, 128), pl.ds(128, 128), pl.ds(0, 256)
     zx_mail = [Mail(pool, 48 + 8 * m, zx_r.at[m]) for m in (0, 1)]
-    zx = []
-    for m, cols in enumerate(chunks):
+    zx = [
+        ring_gather(dp, t, xs, ((every, cols), (low, cols), (high, cols)), zx_mail[m])
+        for m, cols in enumerate(chunks)
+    ]
+
+    def arrive(m):
+        cols = chunks[m]
         hops[1][m][1]()
         part = rv2[:, :, cols].reshape(NDP * TOK, cols.size)
         xs[t, :, cols] = dot(to_work, part).astype(BF)
-        zx.append(
-            ring_gather(dp, t, xs, ((every, cols), (low, cols), (high, cols)), zx_mail[m])
-        )
-        next(zx[m])
+
+    arrive(0)
+    step(zx[:1])
+    step(gathers[:2])
+    arrive(1)
 
     seg = iota((NTOK, FEAT), 1) // 160
     square = xs[t].astype(F32)
@@ -475,15 +490,14 @@
         part = jnp.sum(jnp.where(seg == p, square, 0.0), axis=1, keepdims=True)
         sums_of = jnp.where(lane == p, part, sums_of)
     sq[t] = sums_of.T[:8]
-
     for k in range(1, NZ):
         push(sq.at[t], sq.at[t], sq_s, (dp, lax.rem(t + k, NZ))).start()
     seven = push(sq.at[pl.ds(0, NZ - 1)], sq.at[pl.ds(0, NZ - 1)], sq_s, sibling)
-    step(gathers)
-    step(gathers)
-    all_gain = gain[...].reshape(1, DM)
-    for k in range(NZ):
-        gains[k] = jnp.concatenate([all_gain[:, 160 * k : 160 * k + 160]] * 4, axis=1)
+    step(zx[1:])
+
+    step(zx)
+    step(gathers[:2])
+    step(gathers[2:])
     seven.wait_recv()
     scale = lax.rsqrt(jnp.sum(sq[...], axis=0) * (1.0 / DM) + 1e-06)
     scale = jnp.concatenate([scale] * 16, axis=0).T
@@ -499,14 +513,10 @@
 
     normalise(0)
     step(zx)
-    step(gathers)
+    step(gathers[:2])
     normalise(-1)
     normalise(1)
-    step(zx)
-    step(gathers)
-    normalise(-2)
-    normalise(2)
-    step(gathers)
+    step(gathers[:2])
 
     def second_rows(k):
         two = lax.rem(k, 2) * 2
@@ -537,7 +547,12 @@
         w = f1[lax.div(j, 2), lax.rem(j, 2)].reshape(FEAT, HID)
         return dot(xn[j], w)
 
+    step(gathers[2:])
     step(zx)
+    normalise(-2)
+    normalise(2)
+    step(gathers[2:])
+    step(zb)
     normalise(-3)
     normalise(3)
     meta_sent()
@@ -545,64 +560,52 @@
     for n in (0, 1):
         for m in (0, 1):
             hops[n][m][2]()
-    step(zb)
-    z1 = first_part(0) + first_part(-1) + first_part(1) + first_part(-2)
-    step(zb)
+    step(gathers[2:])
     for m in ag_mail:
         m.finish()
+    z1 = first_part(0) + first_part(-1) + first_part(1) + first_part(-2)
     z1 = z1 + first_part(2) + first_part(-3) + first_part(3)
     step(zx)
     normalise(4)
+    for xx in range(4):
+        core_mail.send(xn.at[xx * 2 + 1 - c], x2.at[xx], 10 + xx, sibling)
     z1 = z1 + first_part(4)
     z1 = jnp.concatenate([z1, jnp.zeros((NTOK, HPAD - HID), F32)], axis=1).T[:HID]
     cdf = 0.5 * (1.0 + lax.erf(z1 * 0.7071067811865476))
-    hid[t] = (z1 * cdf).astype(BF)
+    hid[t] = (z1 * cdf).astype(BF).reshape(2, 2, 80, NTOK)
 
     zh_mail = [Mail(pool, 8 * m, zh_r.at[m]) for m in (0, 1)]
+    full = slice(None)
     zh = [
         ring_gather(
             dp, t, hid,
-            ((pl.ds(0, 320), cut), (pl.ds(0, 160), cut), (pl.ds(160, 160), cut)),
+            ((full, full, full, cut), (pl.ds(0, 1), full, full, cut), (pl.ds(1, 1), full, full, cut)),
             zh_mail[m],
         )
         for m, cut in enumerate(tokens)
     ]
-    core_mail = Mail(pool, 96, co_r)
-    sent = []
-
-    def use_hidden(k):
-        j = turn(t, k, NZ)
-        yy, two = lax.div(j, 2), pl.ds(lax.rem(j, 2) * 2, 2)
-        p2[yy, two] = dot(hid[j], up_rows[...]).astype(BF).reshape(2, 2, 80, OUT)
-        core_mail.send(p2.at[yy, two, 1 - c], b_cores.at[yy, two], len(sent), sibling)
-        sent.append((yy, two))
-
-    summed = []
-
-    def join_cores():
-        while len(summed) < len(sent):
-            yy, two = sent[len(summed)]
-            core_mail.wait(b_cores.at[yy, two], len(summed), sibling)
-            mine = p2.at[yy, two, c]
-            mine[...] = (mine[...].astype(F32) + b_cores[yy, two].astype(F32)).astype(BF)
-            summed.append(yy)
-
-    def grad1(xx, cc):
-        term = dot(xn[xx * 2 + cc], dz[:, :HID], 0, 0).astype(BF)
-        p1[xx, cc] = term.reshape(4, 160, HID)
-
-    step(zh)
-    step(zb)
-    slope = cdf + z1 * (jnp.exp(-0.5 * z1 * z1) * 0.3989422804014327)
-    step(zb)
-    dz_t = acc[...] * slope
-    dz[...] = jnp.concatenate([dz_t, jnp.zeros((HPAD - HID, NTOK), F32)], axis=0).T.astype(BF)
-    for xx in range(4):
-        grad1(xx, 1 - c)
-        core_mail.send(p1.at[xx, 1 - c], a_cores.at[xx], 8 + xx, sibling)
-    use_hidden(0)
-    for m in zx_mail:
-        m.finish()
+    order = (0, -1, 1, -2, 2, -3, 3, 4)
+
+    def share(*ks):
+        for k in ks:
+            j = turn(t, k, NZ)
+            core_mail.send(hid.at[j, :, 1 - c], hid2.at[j], order.index(k), sibling)
+
+    def use_hidden(*ks):
+        for k in ks:
+            j = turn(t, k, NZ)
+            mine = dot(hid[j, :, c].reshape(160, NTOK), up_rows[...])
+            core_mail.wait(hid2.at[j], order.index(k), sibling)
+            term = mine + dot(hid2[j].reshape(160, NTOK), up2[...])
+            p2[lax.div(j, 2), pl.ds(lax.rem(j, 2) * 2, 2)] = term.astype(BF).reshape(2, 80, OUT)
+
+    def grad1(xx):
+        mine = dot(xn[xx * 2 + c], dz[:, :HID], 0, 0)
+        if xx == 0:
+            core_mail.wait(dz2, 9, sibling)
+        core_mail.wait(x2.at[xx], 10 + xx, sibling)
+        p1[xx] = (mine + dot(x2[xx], dz2[:, :HID], 0, 0)).astype(BF).reshape(4, 160, HID)
+
     rs_mail = [Mail(pool, (56, 76, 16, 36)[n], rs_r.at[n]) for n in range(4)]
 
     def put2(h):
@@ -628,41 +631,48 @@
             room = (a_sub0.at[h], a_sub1.at[h], a_full.at[h],
                     a_last0.at[h], a_last1.at[h], a_last.at[h])
             sums.append(ring_sums(hf, p1, room, rs_mail[n], put1(h)))
+    def forward(k):
+        return dot(hid[k].reshape(HID, NTOK), second_rows(k), 0, 0)
+
     step(zh)
+    share(0)
+    step(zb)
+    slope = cdf + z1 * (jnp.exp(-0.5 * z1 * z1) * 0.3989422804014327)
+    core_mail.wait(up2, 8, sibling)
+    use_hidden(0)
+    step(zh)
+    share(-1, 1)
+    step(zb)
+    use_hidden(-1, 1)
+    step(zh)
+    share(-2, 2)
+    step(zb)
+    dz_t = acc[...] * slope
+    dz[...] = jnp.concatenate([dz_t, jnp.zeros((HPAD - HID, NTOK), F32)], axis=0).T.astype(BF)
+    core_mail.send(dz, dz2, 9, sibling)
+    use_hidden(-2, 2)
+    for m in zx_mail:
+        m.finish()
+    step(zh)
+    share(-3, 3)
     for xx in range(4):
-        grad1(xx, c)
-        core_mail.wait(a_cores.at[xx], 8 + xx, sibling)
-        mine = p1.at[xx, c]
-        mine[...] = (mine[...].astype(F32) + a_cores[xx].astype(F32)).astype(BF)
+        grad1(xx)
     step(sums[2:])
-    use_hidden(-1)
-    use_hidden(1)
-    step(zh)
-    use_hidden(-2)
-    use_hidden(2)
-    join_cores()
-    step(sums[2:])
-    step(zh)
-    use_hidden(-3)
-    use_hidden(3)
-    join_cores()
+    use_hidden(-3, 3)
     for m in zb_mail:
         m.finish()
+    step(zh)
+    share(4)
     step(sums[2:])
-    step(zh)
     use_hidden(4)
-    join_cores()
     step(sums[:2])
     step(sums[2:])
-
-    def forward(k):
-        return dot(hid[k], second_rows(k), 0, 0)
-
     mixed[...] = forward(0) + forward(1) + forward(2) + forward(3)
     step(sums[:2])
     step(sums[2:])
     merged = (mixed[...] + forward(4) + forward(5) + forward(6) + forward(7)).astype(BF)
     step(sums[:2])
+    step(sums[2:])
     text_in.wait()
     covered = jnp.max(place[...].astype(F32), axis=1, keepdims=True) > 0.5
     lm_out[...] = jnp.where(covered, dot(place[...], merged), text[...].astype(F32)).astype(BF)
@@ -704,27 +714,29 @@
         V((NTOK, OUT), BF),
         V((LM, NTOK), BF),
         V((HID, NTOK), F32),
-        V((NZ, HID, NTOK), BF),
+        V((NZ, 2, 2, 80, NTOK), BF),
         V((NZ, HID, NTOK), BF),
         V((8, HID, NTOK), BF),
         V((NTOK, HPAD), BF),
         V((NTOK, OUT), F32),
-        V((4, 2, 4, 160, HID), BF),
-        V((4, 4, 2, 80, OUT), BF),
         V((4, 4, 160, HID), BF),
+        V((4, 4, 80, OUT), BF),
+        V((NZ, 2, 80, NTOK), BF),
+        V((NTOK, OUT), BF),
+        V((NTOK, HPAD), BF),
+        V((4, NTOK, FEAT), BF),
         V((2, 4, 48, HID), BF),
         V((2, 4, 32, HID), BF),
         V((2, 2, 4, 80, HID), BF),
         V((2, 48, HID), BF),
         V((2, 32, HID), BF),
         V((2, 2, 80, HID), BF),
-        V((4, 4, 80, OUT), BF),
         V((2, 2, 4, 80, 256), BF),
         V((2, 2, 4, 80, 512), BF),
         V((2, 2, 80, 256), BF),
         V((2, 2, 80, 512), BF),
-        D((108,)), D((2,)), D((2,)), D((4, 2)),
-        D((4, 9)), D((2, 8)), D((2, 8)), D((2, 8)), D((12,)), D((4, 20)),
+        D((110,)), D((2,)), D((2,)), D((4, 2)),
+        D((4, 9)), D((2, 8)), D((2, 8)), D((2, 8)), D((14,)), D((4, 20)),
     ]
     return pl.pallas_call(
         body,

time: 128 us -> 120 us (0.938)
  Pallas kernels: 124 us -> 116 us
    pallas_call x1, Pallas kernels: 124 us -> 116 us  [per_device(): pl.pallas_call(body, out_shape=(pltpu.VMEM((LM, OUT), BF), pltpu.VMEM((16...]
where the time goes in v4:
time: 120 us; the launch traced here: 119 us
  Pallas kernels  116 us (97%)
  local copies, waits for them, and re-layouts  2.39 us (2%)
    pallas_call x1, Pallas kernels, per_device(): pl.pallas_call(body, out_shape=(pltpu.VMEM((LM, OUT), BF), pltpu.VMEM((16...  116 us

profile of v4, /device:TPU:2, one launch (start us, length us, event | category | flops | bytes accessed | tf_op | source)
XLA Modules:
  0.0 119.0 jit_solution(11408933937261917997)
XLA Ops:
  0.6 116.0 %shard_map.103 = (bf16[512,1024]{1,0:T(8,128)(2,1)S(1)}, f32[160,320]{1,0:T(8,128)S(1)}, f32[80,1024]{1,0:T(8,128)S(1)}) custom-call(bf16[160,1536]{1,0:T(8,128)(2,1)} %bitcast.1, f32[1280]{0:T(1024)} %gain.1, s32[24]{0:T(128)} %dest.1, s32[24]{0:T(128)} %pos.1, bf16[160,320]{1,0:T(8,128)(2,1)} %fc1.1, bf16[80,1024]{1,0:T(8,128)(2,1)} %fc2.1, ...), custom_call_target="tpu_custom_call" | custom-call | flops 6000000000 | bytes 8000000 | tf_op jit(solution)/shard_map/pallas_call | solution.py:741
  116.6 1.0 copy.14
  117.6 0.7 copy.15
  118.3 0.7 copy.16

commit v5 on v4

--- a/solution.py
+++ b/solution.py
@@ -96,65 +96,61 @@
 
 
 class Mail:
-    def __init__(self, pool, first, recv):
-        self.pool, self.next, self.r, self.started = pool, first, recv, []
-
-    def make(self, src, dst, send, i, device):
+    def __init__(self, pool, first, recv, *totals):
+        self.pool, self.first, self.r, self.totals = pool, first, recv, totals
+
+    def make(self, src, dst, lot, i, device):
         return pltpu.make_async_remote_copy(
             src_ref=src,
             dst_ref=dst,
-            send_sem=self.pool.at[send],
+            send_sem=self.pool.at[self.first + lot],
             recv_sem=self.r.at[i],
             device_id=device,
             device_id_type=MESH,
         )
 
-    def send(self, src, dst, i, device):
-        copy = self.make(src, dst, self.next, i, device)
-        copy.start()
-        self.next += 1
-        self.started.append(copy)
+    def send(self, src, dst, i, device, lot=0):
+        self.make(src, dst, lot, i, device).start()
 
     def wait(self, dst, i, device):
         self.make(dst, dst, 0, i, device).wait_recv()
 
-    def finish(self):
-        for copy in self.started:
-            copy.wait_send()
-        self.started = []
+    def finish(self, device):
+        for lot, view in enumerate(self.totals):
+            self.make(view, view, lot, 0, device).wait_send()
 
 
 def plane_gather(hf, buf, mail):
-    def send(ref, i, device):
-        mail.send(ref, ref, i, device)
+    def send(ref, i, device, lot=0):
+        mail.send(ref, ref, i, device, lot)
 
     def wait(ref, i):
         mail.wait(ref, i, hf.sibling())
 
-    send(hf.block(buf, 0), 0, hf.first(1))
-    send(hf.block(buf, 0), 1, hf.first(-1))
+    send(hf.block(buf, 0), 0, hf.first(1), 0)
+    send(hf.block(buf, 0), 1, hf.first(-1), 0)
     yield
     wait(hf.block(buf, -1), 0)
-    send(hf.block(buf, -1, 0), 2, hf.first(1))
+    send(hf.block(buf, -1, 0), 2, hf.first(1), 0)
     wait(hf.block(buf, 1), 1)
-    send(hf.block(buf, 1, 1), 3, hf.first(-1))
+    send(hf.block(buf, 1, 1), 3, hf.first(-1), 0)
     yield
     wait(hf.block(buf, 2, 0), 2)
     wait(hf.block(buf, 2, 1), 3)
-    send(hf.group(buf, 0), 4, hf.second(1))
-    send(hf.group(buf, 0), 5, hf.second(-1))
-    send(hf.group(buf, 0), 6, hf.sibling())
+    send(hf.group(buf, 0), 4, hf.second(1), 2)
+    send(hf.group(buf, 0), 5, hf.second(-1), 2)
+    send(hf.group(buf, 0), 6, hf.sibling(), 2)
     yield
     wait(hf.group(buf, -1), 4)
-    send(hf.group(buf, -1, 0), 7, hf.second(1))
-    send(hf.group(buf, -1), 6, hf.sibling())
+    send(hf.group(buf, -1, 0), 7, hf.second(1), 1)
+    send(hf.group(buf, -1), 6, hf.sibling(), 2)
     wait(hf.group(buf, 1), 5)
-    send(hf.group(buf, 1, 1), 8, hf.second(-1))
-    send(hf.group(buf, 1), 6, hf.sibling())
+    send(hf.group(buf, 1, 1), 8, hf.second(-1), 1)
+    send(hf.group(buf, 1), 6, hf.sibling(), 2)
     yield
     wait(hf.group(buf, 2, 0), 7)
     wait(hf.group(buf, 2, 1), 8)
-    send(hf.group(buf, 2), 6, hf.sibling())
+    send(hf.group(buf, 2), 6, hf.sibling(), 2)
     yield
     wait(hf.at(buf, slice(None), slice(None), 1 - hf.c, None), 6)
     yield
@@ -190,15 +186,15 @@
         wait(full.at[1, n], 12 + n)
         plus(hf.cell(buf, 0, order[n]), full.at[0, n], full.at[1, n])
         if n == 0:
-            mail.send(hf.cell(buf, 0, 2, 0), last0, 16, hf.first(1))
-            mail.send(hf.cell(buf, 0, 2, 1), last1, 17, hf.first(-1))
+            mail.send(hf.cell(buf, 0, 2, 0), last0, 16, hf.first(1), 1)
+            mail.send(hf.cell(buf, 0, 2, 1), last1, 17, hf.first(-1), 1)
     yield
     wait(last0, 16)
     plus(hf.cell(buf, 0, 1, 0), last0)
-    mail.send(hf.cell(buf, 0, 1), last.at[0], 18, hf.first(1))
+    mail.send(hf.cell(buf, 0, 1), last.at[0], 18, hf.first(1), 1)
     wait(last1, 17)
     plus(hf.cell(buf, 0, -1, 1), last1)
-    mail.send(hf.cell(buf, 0, -1), last.at[1], 19, hf.first(-1))
+    mail.send(hf.cell(buf, 0, -1), last.at[1], 19, hf.first(-1), 1)
     yield
     wait(full.at[0, 3], 11)
     wait(full.at[1, 3], 15)
@@ -206,6 +202,60 @@
     wait(last.at[1], 19)
     total = hf.cell(buf, 0, 0)[...].astype(F32)
     for part in (full[0, 3], full[1, 3], last[0], last[1]):
+        total = total + part.astype(F32)
+    put(total)
+    yield
+
+
+def group_sums(hf, buf, room, mail, put):
+    sub0, sub1, full, last0, last1, last = room
+
+    def wait(ref, i):
+        mail.wait(ref, i, hf.sibling())
+
+    def row(g, s=None):
+        rows, cols = hf.cut(s)
+        p = turn(hf.r, g, 4)
+        if hf.h == 0:
+            return buf.at[:, p, rows, cols]
+        return buf.at[p, :, rows, cols]
+
+    def plus(mine, *others):
+        total = mine[...].astype(F32)
+        for o in others:
+            total = total + o[...].astype(F32)
+        mine[...] = total.astype(BF)
+
+    mail.send(row(2, 0), sub0, 0, hf.second(1))
+    mail.send(row(2, 1), sub1, 1, hf.second(-1))
+    yield
+    wait(sub0, 0)
+    plus(row(1, 0), sub0)
+    mail.send(row(1), full.at[0], 2, hf.second(1))
+    wait(sub1, 1)
+    plus(row(-1, 1), sub1)
+    mail.send(row(-1), full.at[1], 3, hf.second(-1))
+    yield
+    wait(full.at[0], 2)
+    wait(full.at[1], 3)
+    for b in (2, 1, -1):
+        q = turn(hf.q, b, 4)
+        plus(hf.cell(buf, 0, b), full.at[0, q], full.at[1, q])
+        if b == 2:
+            mail.send(hf.cell(buf, 0, 2, 0), last0, 4, hf.first(1), 1)
+            mail.send(hf.cell(buf, 0, 2, 1), last1, 5, hf.first(-1), 1)
+    yield
+    wait(last0, 4)
+    plus(hf.cell(buf, 0, 1, 0), last0)
+    mail.send(hf.cell(buf, 0, 1), last.at[0], 6, hf.first(1), 1)
+    wait(last1, 5)
+    plus(hf.cell(buf, 0, -1, 1), last1)
+    mail.send(hf.cell(buf, 0, -1), last.at[1], 7, hf.first(-1), 1)
+    yield
+    wait(last.at[0], 6)
+    wait(last.at[1], 7)
+    total = hf.cell(buf, 0, 0)[...].astype(F32)
+    for part in (full[0, hf.q], full[1, hf.q], last[0], last[1]):
         total = total + part.astype(F32)
     put(total)
     yield
@@ -285,7 +335,7 @@
     acc, hid, hb, hb_room, dz, mixed, p1, p2, hid2, up2, dz2, x2,
     a_sub0, a_sub1, a_full, a_last0, a_last1, a_last,
     b_sub, b_full, b_lasts, b_last,
-    pool, sq_s, meta_s, hop_s, ag_r, zx_r, zh_r, zb_r, co_r, rs_r,
+    pool, sq_s, meta_s, hop_s, ag_r, zx_r, zh_r, zb_r, co_r, rs_r, rs_q,
 ):
     dp = lax.axis_index("dp")
     t = lax.axis_index("tensor")
@@ -398,7 +448,16 @@
     hops[0][1][0]()
 
     halves = [Half(kind, h, y, x, c, t) for kind in (2, 1) for h in (0, 1)]
-    ag_mail = [Mail(pool, 12 * n, ag_r.at[n]) for n in range(4)]
+    ag_mail = []
+    for n, hf in enumerate(halves):
+        buf = f2 if hf.kind == 2 else f1
+        three, all4 = pl.ds(0, 3), slice(None)
+        ag_mail.append(
+            Mail(
+                pool, 3 * n, ag_r.at[n],
+                hf.at(buf, 0, three, 0, None), hf.at(buf, 0, all4, 0, None), hf.at(buf, all4, three, all4, None),
+            )
+        )
     gathers = [
         plane_gather(hf, f2 if hf.kind == 2 else f1, m) for hf, m in zip(halves, ag_mail)
     ]
@@ -457,14 +516,17 @@
     step(gathers)
     lmg_in.wait()
     up_rows[...] = dot(fetch, lmg[...]).astype(BF)
-    core_mail = Mail(pool, 96, co_r)
-    core_mail.send(up_rows, up2, 8, sibling)
+    core_mail = Mail(pool, 18, co_r, hid2, up_rows, dz, x2)
+    core_mail.send(up_rows, up2, 8, sibling, 1)
     all_gain = gain[...].reshape(1, DM)
     for k in range(NZ):
         gains[k] = jnp.concatenate([all_gain[:, 160 * k : 160 * k + 160]] * 4, axis=1)
 
     low, high, every = pl.ds(0, 128), pl.ds(128, 128), pl.ds(0, 256)
-    zx_mail = [Mail(pool, 48 + 8 * m, zx_r.at[m]) for m in (0, 1)]
+    seven_of = pl.ds(0, 7)
+    zx_mail = [
+        Mail(pool, 12 + m, zx_r.at[m], xs.at[seven_of, :, cols]) for m, cols in enumerate(chunks)
+    ]
     zx = [
         ring_gather(dp, t, xs, ((every, cols), (low, cols), (high, cols)), zx_mail[m])
         for m, cols in enumerate(chunks)
@@ -514,6 +576,7 @@
     normalise(0)
     step(zx)
     step(gathers[:2])
+    step(gathers[2:])
     normalise(-1)
     normalise(1)
     step(gathers[:2])
@@ -522,14 +585,15 @@
         two = lax.rem(k, 2) * 2
         return f2[lax.div(k, 2), pl.ds(two, 2)].reshape(HID, OUT)
 
-    def back(k, carry):
-        hb[k] = dot(second_rows(k), up_rows[...], 1, 1).astype(BF)
-        return carry
-
-    lax.fori_loop(0, NZ, back, 0)
+    def back(*ks):
+        for k in ks:
+            j = turn(t, k, NZ)
+            hb[j] = dot(second_rows(j), up_rows[...], 1, 1).astype(BF)
 
     tokens = (low, high)
-    zb_mail = [Mail(pool, 64 + 8 * m, zb_r.at[m]) for m in (0, 1)]
+    zb_mail = [
+        Mail(pool, 14 + m, zb_r.at[m], hb.at[seven_of, :, cut]) for m, cut in enumerate(tokens)
+    ]
 
     def put_back(m):
         def put(total):
@@ -540,14 +604,15 @@
     zb = [
         ring_scatter(dp, t, hb, hb_room, tokens[m], zb_mail[m], put_back(m)) for m in (0, 1)
     ]
+    back(4)
     step(zb)
+    back(3, -3, 2, -2, 1, -1, 0)
 
     def first_part(k):
         j = turn(t, k, NZ)
         w = f1[lax.div(j, 2), lax.rem(j, 2)].reshape(FEAT, HID)
         return dot(xn[j], w)
 
-    step(gathers[2:])
     step(zx)
     normalise(-2)
     normalise(2)
@@ -561,20 +626,20 @@
         for m in (0, 1):
             hops[n][m][2]()
     step(gathers[2:])
-    for m in ag_mail:
-        m.finish()
     z1 = first_part(0) + first_part(-1) + first_part(1) + first_part(-2)
     z1 = z1 + first_part(2) + first_part(-3) + first_part(3)
     step(zx)
     normalise(4)
     for xx in range(4):
-        core_mail.send(xn.at[xx * 2 + 1 - c], x2.at[xx], 10 + xx, sibling)
+        core_mail.send(xn.at[xx * 2 + 1 - c], x2.at[xx], 10 + xx, sibling, 3)
     z1 = z1 + first_part(4)
     z1 = jnp.concatenate([z1, jnp.zeros((NTOK, HPAD - HID), F32)], axis=1).T[:HID]
     cdf = 0.5 * (1.0 + lax.erf(z1 * 0.7071067811865476))
     hid[t] = (z1 * cdf).astype(BF).reshape(2, 2, 80, NTOK)
 
-    zh_mail = [Mail(pool, 8 * m, zh_r.at[m]) for m in (0, 1)]
+    zh_mail = [
+        Mail(pool, 16 + m, zh_r.at[m], hid.at[seven_of, :, :, :, cut]) for m, cut in enumerate(tokens)
+    ]
     full = slice(None)
     zh = [
         ring_gather(
@@ -606,7 +671,16 @@
         core_mail.wait(x2.at[xx], 10 + xx, sibling)
         p1[xx] = (mine + dot(x2[xx], dz2[:, :HID], 0, 0)).astype(BF).reshape(4, 160, HID)
 
-    rs_mail = [Mail(pool, (56, 76, 16, 36)[n], rs_r.at[n]) for n in range(4)]
+    rs_mail = []
+    for n, hf in enumerate(halves):
+        buf = p2 if hf.kind == 2 else p1
+        rows, cols = hf.cut(None)
+        rs_mail.append(
+            Mail(
+                pool, 22 + 2 * n, (rs_r if hf.kind == 2 else rs_q).at[hf.h],
+                buf.at[:, three, rows, cols], buf.at[0, three, rows, cols],
+            )
+        )
 
     def put2(h):
         def put(total):
@@ -630,7 +704,7 @@
         else:
             room = (a_sub0.at[h], a_sub1.at[h], a_full.at[h],
                     a_last0.at[h], a_last1.at[h], a_last.at[h])
-            sums.append(ring_sums(hf, p1, room, rs_mail[n], put1(h)))
+            sums.append(group_sums(hf, p1, room, rs_mail[n], put1(h)))
     def forward(k):
         return dot(hid[k].reshape(HID, NTOK), second_rows(k), 0, 0)
 
@@ -649,18 +723,14 @@
     step(zb)
     dz_t = acc[...] * slope
     dz[...] = jnp.concatenate([dz_t, jnp.zeros((HPAD - HID, NTOK), F32)], axis=0).T.astype(BF)
-    core_mail.send(dz, dz2, 9, sibling)
+    core_mail.send(dz, dz2, 9, sibling, 2)
     use_hidden(-2, 2)
-    for m in zx_mail:
-        m.finish()
     step(zh)
     share(-3, 3)
     for xx in range(4):
         grad1(xx)
     step(sums[2:])
     use_hidden(-3, 3)
-    for m in zb_mail:
-        m.finish()
     step(zh)
     share(4)
     step(sums[2:])
@@ -678,13 +748,11 @@
     lm_out[...] = jnp.where(covered, dot(place[...], merged), text[...].astype(F32)).astype(BF)
     lm_done.start()
     step(sums[:2])
-    for m in zh_mail + [core_mail]:
-        m.finish()
     step(sums[:2])
 
     lm_done.wait()
-    for m in rs_mail:
-        m.finish()
+    for m in ag_mail + zx_mail + zb_mail + zh_mail + [core_mail] + rs_mail:
+        m.finish(sibling)
 
 
 def per_device(patches, gain, window_dest, window_pos, fc1, fc2, text_embeds, lm_grad):
@@ -735,8 +803,8 @@
         V((2, 2, 4, 80, 512), BF),
         V((2, 2, 80, 256), BF),
         V((2, 2, 80, 512), BF),
-        D((110,)), D((2,)), D((2,)), D((4, 2)),
-        D((4, 9)), D((2, 8)), D((2, 8)), D((2, 8)), D((14,)), D((4, 20)),
+        D((30,)), D((2,)), D((2,)), D((4, 2)),
+        D((4, 9)), D((2, 8)), D((2, 8)), D((2, 8)), D((14,)), D((2, 20)), D((2, 8)),
     ]
     return pl.pallas_call(
         body,

time: 120 us -> 119 us (level)
  no operation moved by 1% of the time
where the time goes in v5:
time: 119 us; the launch traced here: 118 us
  Pallas kernels  115 us (97%)
  local copies, waits for them, and re-layouts  2.39 us (2%)
    pallas_call x1, Pallas kernels, per_device(): pl.pallas_call(body, out_shape=(pltpu.VMEM((LM, OUT), BF), pltpu.VMEM((16...  115 us
    unnamed x3, local copies, waits for them, and re-layouts  2.39 us

profile of v5, /device:TPU:2, one launch (start us, length us, event | category | flops | bytes accessed | tf_op | source)
XLA Modules:
  0.0 118.3 jit_solution(1068033748493673978)
XLA Ops:
  0.6 115.3 %shard_map.103 = (bf16[512,1024]{1,0:T(8,128)(2,1)S(1)}, f32[160,320]{1,0:T(8,128)S(1)}, f32[80,1024]{1,0:T(8,128)S(1)}) custom-call(bf16[160,1536]{1,0:T(8,128)(2,1)} %bitcast.1, f32[1280]{0:T(1024)} %gain.1, s32[24]{0:T(128)} %dest.1, s32[24]{0:T(128)} %pos.1, bf16[160,320]{1,0:T(8,128)(2,1)} %fc1.1, bf16[80,1024]{1,0:T(8,128)(2,1)} %fc2.1, ...), custom_call_target="tpu_custom_call" | custom-call | flops 6000000000 | bytes 8000000 | tf_op jit(solution)/shard_map/pallas_call | solution.py:809
  115.9 1.0 copy.14
  116.9 0.7 copy.15
  117.6 0.7 copy.16

commit v6 on v5

--- a/solution.py
+++ b/solution.py
@@ -328,9 +328,9 @@
 
 
 def body(
-    patches_t, gain, dest, pos, fc1, fc2, text_hbm, lmg_hbm,
+    patches_hbm, gain, dest, pos, fc1, fc2, text_hbm, lmg_hbm,
     lm_hbm, g1_out, g2_out,
-    text, lmg, lm_out, io_s,
+    patches_t, text, lmg, lm_out, io_s,
     sq, meta, gains, factor, xn, flat, st1, rv1, st2, rv2, xs, f1, f2, up_rows, place,
     acc, hid, hb, hb_room, dz, mixed, p1, p2, hid2, up2, dz2, x2,
     a_sub0, a_sub1, a_full, a_last0, a_last1, a_last,
@@ -364,16 +364,17 @@
 
     lax.fori_loop(1, NZ, greet_z, 0)
 
-    lmg_in.start()
-    text_in.start()
+    patches_in = pltpu.make_async_copy(patches_hbm, patches_t, io_s.at[3])
+    fc2_in = pltpu.make_async_copy(fc2, f2.at[y, x, c], io_s.at[4])
+    fc1_in = pltpu.make_async_copy(fc1, f1.at[x, c, y], io_s.at[5])
+    for copy in (patches_in, fc2_in, fc1_in, lmg_in, text_in):
+        copy.start()
 
     q = iota((1, 128), 1)
     table = jnp.full((1, 128), -1, jnp.int32)
     for s in range(SRC):
         table = jnp.where(q == s, jnp.where(dest[s] >= 0, (dest[s] << 14) + pos[s], -1), table)
     meta[dp] = table
-    f2[y, x, c] = fc2[...]
-    f1[x, c, y] = fc1[...]
 
     def selector(count, key):
         n = key.shape[1]
@@ -387,6 +388,7 @@
             jnp.where(iota((k, n), 0) == (iota((k, n), 1) >> 4), column, 0.0), axis=0, keepdims=True
         )
 
+    patches_in.wait()
     value = patches_t[...].astype(F32)
     flat[0] = value[:128].T
     flat[1] = jnp.concatenate([value[128:], jnp.zeros((96, SRC * WIN), F32)], axis=0).T
@@ -448,6 +450,8 @@
     hops[0][1][0]()
 
     halves = [Half(kind, h, y, x, c, t) for kind in (2, 1) for h in (0, 1)]
+    fc2_in.wait()
+    fc1_in.wait()
     ag_mail = []
     for n, hf in enumerate(halves):
         buf = f2 if hf.kind == 2 else f1
@@ -733,7 +737,6 @@
     use_hidden(-3, 3)
     step(zh)
     share(4)
-    step(sums[2:])
     use_hidden(4)
     step(sums[:2])
     step(sums[2:])
@@ -748,6 +751,7 @@
     lm_out[...] = jnp.where(covered, dot(place[...], merged), text[...].astype(F32)).astype(BF)
     lm_done.start()
     step(sums[:2])
+    step(sums[2:])
     step(sums[:2])
 
     lm_done.wait()
@@ -762,10 +766,11 @@
     V = pltpu.VMEM
     D = pltpu.SemaphoreType.DMA
     scratch = [
+        V((160, SRC * WIN), BF),
         V((LM, OUT), BF),
         V((LM, OUT), BF),
         V((LM, OUT), BF),
-        D((3,)),
+        D((6,)),
         V((NZ, 8, NTOK), F32),
         V((NDP, 1, 128), jnp.int32),
         V((NZ, 1, FEAT), F32),
@@ -813,7 +818,7 @@
             pltpu.VMEM((160, HID), F32),
             pltpu.VMEM((80, OUT), F32),
         ),
-        in_specs=[vm, vm, sm, sm, vm, vm, anywhere, anywhere],
+        in_specs=[anywhere, vm, sm, sm] + [anywhere] * 4,
         out_specs=(anywhere, vm, vm),
         scratch_shapes=scratch,
         compiler_params=pltpu.CompilerParams(

time: 119 us -> 117 us (0.983)
  Pallas kernels: 115 us -> 112 us
    pallas_call x1, Pallas kernels: 115 us -> 112 us  [per_device(): pl.pallas_call(body, out_shape=(pltpu.VMEM((LM, OUT), BF), pltpu.VMEM((16...]
where the time goes in v6:
time: 117 us; the launch traced here: 115 us
  Pallas kernels  112 us (96%)
  local copies, waits for them, and re-layouts  2.39 us (2%)
    pallas_call x1, Pallas kernels, per_device(): pl.pallas_call(body, out_shape=(pltpu.VMEM((LM, OUT), BF), pltpu.VMEM((16...  112 us
    unnamed x3, local copies, waits for them, and re-layouts  2.39 us

profile of v6, /device:TPU:2, one launch (start us, length us, event | category | flops | bytes accessed | tf_op | source)
XLA Modules:
  0.0 115.4 jit_solution(6498027948865119836)
XLA Ops:
  0.6 112.3 %shard_map.103 = (bf16[512,1024]{1,0:T(8,128)(2,1)S(1)}, f32[160,320]{1,0:T(8,128)S(1)}, f32[80,1024]{1,0:T(8,128)S(1)}) custom-call(bf16[160,1536]{1,0:T(8,128)(2,1)} %bitcast.1, f32[1280]{0:T(1024)} %gain.1, s32[24]{0:T(128)} %dest.1, s32[24]{0:T(128)} %pos.1, bf16[160,320]{1,0:T(8,128)(2,1)} %fc1.1, bf16[80,1024]{1,0:T(8,128)(2,1)} %fc2.1, ...), custom_call_target="tpu_custom_call" | custom-call | flops 6000000000 | bytes 8000000 | tf_op jit(solution)/shard_map/pallas_call | solution.py:814
  113.0 1.0 copy.14
  114.0 0.7 copy.15
  114.6 0.7 copy.16

commit v7 on v6

--- a/solution.py
+++ b/solution.py
@@ -661,12 +661,16 @@
             core_mail.send(hid.at[j, :, 1 - c], hid2.at[j], order.index(k), sibling)
 
     def use_hidden(*ks):
-        for k in ks:
-            j = turn(t, k, NZ)
-            mine = dot(hid[j, :, c].reshape(160, NTOK), up_rows[...])
+        js = [turn(t, k, NZ) for k in ks]
+        mine = jnp.concatenate([hid[j, :, c].reshape(160, NTOK) for j in js], axis=0)
+        term = dot(mine, up_rows[...])
+        for k, j in zip(ks, js):
             core_mail.wait(hid2.at[j], order.index(k), sibling)
-            term = mine + dot(hid2[j].reshape(160, NTOK), up2[...])
-            p2[lax.div(j, 2), pl.ds(lax.rem(j, 2) * 2, 2)] = term.astype(BF).reshape(2, 80, OUT)
+        theirs = jnp.concatenate([hid2[j].reshape(160, NTOK) for j in js], axis=0)
+        term = (term + dot(theirs, up2[...])).astype(BF)
+        for n, j in enumerate(js):
+            part = term[160 * n : 160 * n + 160].reshape(2, 80, OUT)
+            p2[lax.div(j, 2), pl.ds(lax.rem(j, 2) * 2, 2)] = part
 
     def grad1(xx):
         mine = dot(xn[xx * 2 + c], dz[:, :HID], 0, 0)

time: 117 us -> 117 us (level)
  no operation moved by 1% of the time
where the time goes in v7:
time: 117 us; the launch traced here: 115 us
  Pallas kernels  112 us (96%)
  local copies, waits for them, and re-layouts  2.39 us (2%)
    pallas_call x1, Pallas kernels, per_device(): pl.pallas_call(body, out_shape=(pltpu.VMEM((LM, OUT), BF), pltpu.VMEM((16...  112 us
    unnamed x3, local copies, waits for them, and re-layouts  2.39 us

profile of v7, /device:TPU:2, one launch (start us, length us, event | category | flops | bytes accessed | tf_op | source)
XLA Modules:
  0.0 115.1 jit_solution(11470708015529883431)
XLA Ops:
  0.6 112.0 %shard_map.103 = (bf16[512,1024]{1,0:T(8,128)(2,1)S(1)}, f32[160,320]{1,0:T(8,128)S(1)}, f32[80,1024]{1,0:T(8,128)S(1)}) custom-call(bf16[160,1536]{1,0:T(8,128)(2,1)} %bitcast.1, f32[1280]{0:T(1024)} %gain.1, s32[24]{0:T(128)} %dest.1, s32[24]{0:T(128)} %pos.1, bf16[160,320]{1,0:T(8,128)(2,1)} %fc1.1, bf16[80,1024]{1,0:T(8,128)(2,1)} %fc2.1, ...), custom_call_target="tpu_custom_call" | custom-call | flops 6000000000 | bytes 8000000 | tf_op jit(solution)/shard_map/pallas_call | solution.py:818
  112.7 1.0 copy.14
  113.7 0.7 copy.15
  114.4 0.7 copy.16
